TPU v7x, 128 devices: a whole 4x4x4 slice. The times are simulated.
128 devices in a mesh: pre: 32 (over z, x, core), exp: 4 (over y).
Axes of the slice: x: 4, y: 4, z: 4, core: 2. Of those that a mesh axis runs over, the one named last changes fastest.
Arguments:
- queries: bfloat16 [32, 8, 128, 576], P('pre', None, 'exp')
- draft_latents: bfloat16 [32, 8, 576], P('pre'), may hold values from -6 to 6
- prefix_latents: bfloat16 [8, 16384, 576], P(None, 'pre')
- prefix_of: int32 [32], replicated, may hold values from 0 to 7, as said below
- accepted: int32 [32], replicated, may hold values from 1 to 8
- w_uv: bfloat16 [128, 512, 128], P('exp'), may hold values from -1 to 1
- w_out: bfloat16 [16384, 7168], P('exp', 'pre'), may hold values from -0.1875 to 0.1875
- residual: bfloat16 [256, 7168], P(None, 'pre')
- norm_gain: bfloat16 [7168], P('pre'), may hold values from 0.5 to 1.5
- w_gate_up: bfloat16 [12, 7168, 2, 2048], P('exp', 'pre'), may hold values from -0.0625 to 0.0625
- w_down: bfloat16 [12, 2048, 7168], P('exp', None, 'pre'), may hold values from -0.125 to 0.125
- shared_gate_up: bfloat16 [7168, 2, 2048], P('pre', None, 'exp'), may hold values from -0.0625 to 0.0625
- shared_down: bfloat16 [2048, 7168], P('exp', 'pre'), may hold values from -0.125 to 0.125
- expert_ids: int32 [256, 8], replicated, may hold values from 0 to 11, all different within a row; in each aligned block of 256 rows (0 to 255, 256 to 511, ...) at most 192 rows name the same one
- expert_gates: float32 [256, 8], replicated, may hold values from 0.05 to 0.25
Outputs:
- layer_out: bfloat16 [256, 7168], P(None, 'pre')
Inputs may be any that keep to these rules, and one draw needn't show every extreme that they name: `prefix_of`: every system prompt is named by some request. `expert_ids`: each expert is named by at most 192 of the 256 tokens, a bound that some block reaches.
All inputs are finite; a program needn't handle non-finite values.
Results may differ from a plain program's by a relative error of at most 0.01.
Values may be sent and summed in bfloat16 or wider, within the bound.
No kernel may reach another device: no remote copies, remote signals or barrier semaphores. Data moves between devices by JAX's collectives and lax.ppermute only.
A program may use at most 192 MiB of HBM per device.

v0:
```python
import jax
import jax.numpy as jnp
from jax import lax
from jax.sharding import PartitionSpec as P

D = 7168
LAT = 512
ROPE = 64
HD = 128
DRAFT = 8
EXP_DEV = 3


def silu_product(gate_part, up_part):
    return jax.nn.silu(gate_part) * up_part


def add_block(whole, block, start):
    current = lax.dynamic_slice_in_dim(whole, start, block.shape[0], 0)
    return lax.dynamic_update_slice_in_dim(whole, current + block, start, 0)


def per_device(
    queries,
    draft_latents,
    prefix_latents,
    prefix_of,
    accepted,
    w_uv,
    w_out,
    residual,
    norm_gain,
    w_gate_up,
    w_down,
    shared_gate_up,
    shared_down,
    expert_ids,
    expert_gates,
):
    softmax_scale = (HD + ROPE) ** (-0.5)
    local_req = queries.shape[0]
    gathered = lax.all_gather(queries, "pre", axis=0, tiled=True)
    prefix_rows = jnp.take(prefix_latents, prefix_of, axis=0)
    far_scores = (
        jnp.einsum("rjhc,rkc->rjhk", gathered, prefix_rows, preferred_element_type=jnp.float32)
        * softmax_scale
    )
    causal = jnp.arange(DRAFT)[None, :] <= jnp.arange(DRAFT)[:, None]
    near_scores = (
        jnp.einsum("rjhc,ric->rjhi", queries, draft_latents, preferred_element_type=jnp.float32)
        * softmax_scale
    )
    near_scores = jnp.where(causal[None, :, None, :], near_scores, -jnp.inf)
    start = lax.axis_index("pre") * local_req
    local_top = jnp.max(far_scores, -1)
    own_top = jnp.maximum(
        lax.dynamic_slice_in_dim(local_top, start, local_req, 0), jnp.max(near_scores, -1)
    )
    local_top = lax.dynamic_update_slice_in_dim(local_top, own_top, start, 0)
    row_top = lax.pmax(local_top, "pre")
    far_weight = jnp.exp(far_scores - row_top[..., None]).astype(jnp.bfloat16)
    own_max = lax.dynamic_slice_in_dim(row_top, start, local_req, 0)
    near_weight = jnp.exp(near_scores - own_max[..., None]).astype(jnp.bfloat16)
    weight_sum = jnp.sum(far_weight, -1, dtype=jnp.float32)
    weight_sum = add_block(weight_sum, jnp.sum(near_weight, -1, dtype=jnp.float32), start)
    summed = jnp.einsum(
        "rjhk,rkc->rjhc", far_weight, prefix_rows[..., :LAT], preferred_element_type=jnp.float32
    )
    own_summed = jnp.einsum(
        "rjhi,ric->rjhc", near_weight, draft_latents[..., :LAT], preferred_element_type=jnp.float32
    )
    summed = add_block(summed, own_summed, start)
    up_table = w_uv.astype(jnp.float32)
    summed, weight_sum = (
        lax.psum_scatter(summed, "pre", scatter_dimension=0, tiled=True),
        lax.psum_scatter(weight_sum, "pre", scatter_dimension=0, tiled=True),
    )
    context = summed / weight_sum[..., None]
    own_heads = jnp.einsum(
        "rjhc,hcv->rjhv", context, up_table, precision=lax.Precision.HIGHEST
    ).astype(jnp.bfloat16)
    own_heads = own_heads.reshape(local_req * DRAFT, own_heads.shape[2] * own_heads.shape[3])
    head_out = lax.all_gather(own_heads, "pre", axis=0, tiled=True)
    attention = jnp.dot(head_out, w_out, preferred_element_type=jnp.float32)
    attention = lax.psum(attention, "exp")
    hidden = residual.astype(jnp.float32) + attention
    squares = lax.psum(jnp.sum(hidden * hidden, -1), "pre")
    normed = (
        hidden * lax.rsqrt(squares / D + 1e-06)[:, None] * norm_gain.astype(jnp.float32)
    ).astype(jnp.bfloat16)
    tokens = expert_ids.shape[0]
    capacity = 3 * tokens // 4
    live = (jnp.arange(DRAFT)[None, :] < accepted[:, None]).reshape(tokens).astype(jnp.float32)
    local_experts = lax.axis_index("exp") * EXP_DEV + jnp.arange(EXP_DEV, dtype=jnp.int32)
    chosen = expert_ids[:, :, None] == local_experts[None, None, :]
    routed = jnp.any(chosen, 1)
    weights = jnp.sum(jnp.where(chosen, expert_gates[:, :, None], 0.0), 1) * live[:, None]
    position = jnp.cumsum(routed.astype(jnp.int32), 0) - 1
    slot_hit = routed[:, :, None] & (
        position[:, :, None] == jnp.arange(capacity, dtype=jnp.int32)[None, None, :]
    )
    token_ids = jnp.arange(tokens, dtype=jnp.int32)
    slot_token = jnp.sum(jnp.where(slot_hit, token_ids[:, None, None], 0), 0)
    slot_weight = jnp.sum(jnp.where(slot_hit, weights[:, :, None], 0.0), 0)
    inputs = jnp.take(normed, slot_token, axis=0)
    gate_up = jnp.einsum("ecd,edgf->ecgf", inputs, w_gate_up, preferred_element_type=jnp.float32)
    shared_pair = jnp.einsum(
        "td,dgf->tgf", normed, shared_gate_up, preferred_element_type=jnp.float32
    )
    gate_up, shared_pair = (
        lax.psum_scatter(
            gate_up.astype(jnp.bfloat16), "pre", scatter_dimension=3, tiled=True
        ).astype(jnp.float32),
        lax.psum_scatter(
            shared_pair.astype(jnp.bfloat16), "pre", scatter_dimension=2, tiled=True
        ).astype(jnp.float32),
    )
    activation = silu_product(gate_up[:, :, 0], gate_up[:, :, 1]).astype(jnp.bfloat16)
    shared_act = silu_product(shared_pair[:, 0], shared_pair[:, 1]).astype(jnp.bfloat16)
    activation, shared_act = (
        lax.all_gather(activation, "pre", axis=2, tiled=True),
        lax.all_gather(shared_act, "pre", axis=1, tiled=True),
    )
    expert_out = jnp.einsum("ecf,efd->ecd", activation, w_down, preferred_element_type=jnp.float32)
    spread = jnp.where(
        slot_token[None] == token_ids[:, None, None], slot_weight[None], 0.0
    ).reshape(tokens, -1)
    routed_sum = jnp.dot(
        spread, expert_out.reshape(-1, expert_out.shape[-1]), precision=lax.Precision.HIGHEST
    )
    shared_out = jnp.dot(shared_act, shared_down, preferred_element_type=jnp.float32)
    mixed = lax.psum((routed_sum + shared_out).astype(jnp.bfloat16), "exp").astype(jnp.float32)
    return (hidden + mixed).astype(jnp.bfloat16)


def solution(mesh):
    return jax.shard_map(
        per_device,
        mesh=mesh,
        in_specs=(
            P("pre", None, "exp", None),
            P("pre", None, None),
            P(None, "pre", None),
            P(),
            P(),
            P("exp", None, None),
            P("exp", "pre"),
            P(None, "pre"),
            P("pre"),
            P("exp", "pre", None, None),
            P("exp", None, "pre"),
            P("pre", None, "exp"),
            P("exp", "pre"),
            P(),
            P(),
        ),
        out_specs=P(None, "pre"),
        check_vma=False,
    )
```

profile of v0, /device:TPU:1, one launch (start us, length us, event | category | flops | bytes accessed | tf_op | source)
XLA Modules:
  0.0 803.9 jit_solution(5172849968931614968)
XLA Ops:
  8.0 10.3 %gather_fusion = bf16[32,512,576]{1,2,0:T(8,128)(2,1)} fusion(bf16[8,512,576]{1,2,0:T(8,128)(2,1)} %param.17, s32[1024]{0:T(1024)S(1)} %pad_clamp_fusion.1), kind=kCustom, calls=%fused_computation | custom fusion | bytes 37748864 | tf_op jit(solution)/shard_map/jit(_take)/gather | solution.py:43
  18.4 28.3 %copy.48 = bf16[32,512,576]{2,1,0:T(8,128)(2,1)} copy(bf16[32,512,576]{1,2,0:T(8,128)(2,1)} %gather_fusion) | data formatting | bytes 37748736 | tf_op jit(solution)/shard_map/jit(_take)/gather | solution.py:43
  47.1 18.0 %broadcast_select_fusion = bf16[32,512,576]{2,1,0:T(8,128)(2,1)} fusion(bf16[32,512,576]{2,1,0:T(8,128)(2,1)} %copy.48, pred[32]{0:T(512)(128)(4,1)S(1)} %compare_and_fusion.1), kind=kLoop, calls=%fused_computation.4 | loop fusion | flops 9437184 | bytes 37748768 | tf_op jit(solution)/shard_map/jit(_take)/select_n | solution.py:43
  65.2 6.0 all-gather.4.cloned.1.call-done
  71.2 19.6 %bitcast_reduce_fusion = (f32[32,8,32]{2,1,0:T(8,128)S(1)}, f32[32,512,8,32]{1,3,2,0:T(8,128)}) fusion(bf16[32,8,32,576]{3,2,1,0:T(8,128)(2,1)} %all-gather.4.cloned.1.call-done, bf16[32,512,576]{2,1,0:T(8,128)(2,1)} %broadcast_select_fusion), kind=kOutput, calls=%fused_computation.8 | convolution fusion | flops 4840218624 | bytes 45121536 | tf_op jit(solution)/shard_map/rjhc,rkc->rjhk/dot_general | solution.py:45
  90.9 121.1 %pmax.7 = f32[32,8,32]{2,1,0:T(8,128)S(1)} all-reduce(f32[32,8,32]{2,1,0:T(8,128)S(1)} %fusion.39), channel_id=1, replica_groups=mesh['pre'=32,'exp'=4] {'pre'}, use_global_device_ids=true, to_apply=%region_2.3 | all-reduce | flops 8192 | bytes 65536 | tf_op jit(solution)/shard_map/pmax | solution.py:60
  212.0 18.9 %fusion.2 = f32[32,8,32,512]{3,2,1,0:T(8,128)} fusion(bf16[32,512,576]{2,1,0:T(8,128)(2,1)} %broadcast_select_fusion, f32[32,512,8,32]{1,3,2,0:T(8,128)} %get-tuple-element.6, f32[32,8,32]{2,1,0:T(8,128)S(1)} %pmax.7), kind=kOutput, calls=%fused_computation.6 | convolution fusion | flops 4307550208 | bytes 50364416 | tf_op jit(solution)/shard_map/rjhk,rkc->rjhc/dot_general | solution.py:66
  230.9 2.1 fusion.11
  233.7 8.0 convert_reduce_fusion
  241.7 126.1 %all-reduce = f32[32,8,32]{2,1,0:T(8,128)S(1)} all-reduce(f32[32,8,32]{2,1,0:T(8,128)S(1)} %fusion.38), channel_id=3, replica_groups=mesh['pre'=32,'exp'=4] {'pre'}, use_global_device_ids=true, to_apply=%region_6.7.clone | all-reduce | flops 8192 | bytes 65536
  368.5 1.1 divide_bitcast_fusion
  369.7 4.4 fusion.14
  374.3 0.9 reduce-window.6
  375.9 43.9 %all-gather.6.cloned.1.call-done = bf16[256,4096]{1,0:T(8,128)(2,1)} async-done(((bf16[8,4096]{1,0:T(8,128)(2,1)}), bf16[256,4096]{1,0:T(8,128)(2,1)}) %all-gather.6.cloned.1.call-update) | async-done | bytes 2097168 | tf_op jit(solution)/shard_map/all_gather | solution.py:83
  419.8 3.6 fusion.44
  423.5 38.4 %all-reduce.4.cloned.1.call-done = f32[256,224]{0,1:T(8,128)} async-done(((f32[256,224]{0,1:T(8,128)}), f32[256,224]{0,1:T(8,128)}) %all-reduce.4.cloned.1.call-update) | async-done | bytes 229392 | tf_op jit(solution)/shard_map/psum | solution.py:85
  461.9 1.1 multiply_reduce_fusion
  463.0 65.1 %psum.22 = f32[256]{0:T(256)S(1)} all-reduce(f32[256]{0:T(256)S(1)} %multiply_reduce_fusion), channel_id=1, replica_groups=mesh['pre'=32,'exp'=4] {'pre'}, use_global_device_ids=true, to_apply=%region_15.16 | all-reduce | flops 256 | bytes 2048 | tf_op jit(solution)/shard_map/psum | solution.py:87
  528.1 1.0 multiply_convert_fusion
  529.3 2.7 gather_fusion.1
  532.0 8.3 %fusion.7 = bf16[3,192,2,2048]{1,3,2,0:T(8,128)(2,1)} fusion(bf16[3,224,2,2048]{3,2,1,0:T(2,128)(2,1)} %param.24, bf16[3,192,224]{2,1,0:T(8,128)(2,1)S(1)} %bitcast.123, pred[3,192]{1,0:T(4,128)(4,1)S(1)} %compare_and_fusion), kind=kOutput, calls=%fused_computation.14 | convolution fusion | flops 1059452928 | bytes 10482240 | tf_op jit(solution)/shard_map/ecd,edgf->ecgf/dot_general | solution.py:106
  540.4 2.2 convolution_convert_fusion
  542.6 80.5 %reduce-scatter.6.cloned.1.call-done = bf16[3,192,2,64]{1,3,2,0:T(8,128)(2,1)} async-done(((bf16[3,192,2,2048]{1,3,2,0:T(8,128)(2,1)}), bf16[3,192,2,64]{1,3,2,0:T(8,128)(2,1)}) %reduce-scatter.6.cloned.1.call-update) | async-done | bytes 147472 | tf_op jit(solution)/shard_map/reduce_scatter | solution.py:111
  623.1 1.0 convert_element_type.93
  626.7 76.2 %reduce-scatter.8.cloned.1.call-done = bf16[256,2,16]{0,2,1:T(8,128)(2,1)} async-done(((bf16[256,2,512]{0,2,1:T(8,128)(2,1)}), bf16[256,2,16]{0,2,1:T(8,128)(2,1)}) %reduce-scatter.8.cloned.1.call-update) | async-done | bytes 16400 | tf_op jit(solution)/shard_map/reduce_scatter | solution.py:114
  703.6 26.3 %all_gather.15 = bf16[256,512]{0,1:T(8,128)(2,1)S(1)} all-gather(bf16[256,16]{0,1:T(8,128)(2,1)S(1)} %fusion.33), channel_id=1, replica_groups=mesh['pre'=32,'exp'=4] {'pre'}, dimensions={1}, use_global_device_ids=true | all-gather | bytes 270336 | tf_op jit(solution)/shard_map/all_gather | solution.py:122
  729.9 21.8 %all-gather.8.cloned.1.call-done = bf16[3,192,2048]{1,2,0:T(8,128)(2,1)} async-done(((bf16[3,192,64]{1,2,0:T(8,128)(2,1)}), bf16[3,192,2048]{1,2,0:T(8,128)(2,1)}) %all-gather.8.cloned.1.call-update) | async-done | bytes 2359312 | tf_op jit(solution)/shard_map/all_gather | solution.py:121
  751.7 3.1 fusion.45
  754.8 1.4 convolution_bitcast_fusion.1
  756.3 1.8 fusion.13
  758.1 37.4 %all-reduce.6.cloned.1.call-done = bf16[256,224]{0,1:T(8,128)(2,1)} async-done(((bf16[256,224]{0,1:T(8,128)(2,1)}), bf16[256,224]{0,1:T(8,128)(2,1)}) %all-reduce.6.cloned.1.call-update) | async-done | bytes 114704 | tf_op jit(solution)/shard_map/psum | solution.py:132
  795.5 1.6 add_convert_fusion
  (75 shorter events, 7.8 us)
Async XLA Ops:
  6.5 745.2 %copy-start = (bf16[3,2048,224]{1,2,0:T(8,128)(2,1)S(1)}, bf16[3,2048,224]{1,2,0:T(8,128)(2,1)}, u32[]{:S(2)}) copy-start(bf16[3,2048,224]{1,2,0:T(8,128)(2,1)} %param.25) | copy-start | bytes 8257540
  6.5 64.7 %all-gather.4.cloned.1.call-start = ((), (), s32[]{:S(2)}) async-start(), calls=%async_computation.3 | async-start | bytes 10813440 | tf_op jit(solution)/shard_map/all_gather | solution.py:42
  7.3 361.3 %reduce-scatter.4.cloned.1.call-start = ((), (), s32[]{:S(2)}) async-start(), calls=%async_computation.4 | async-start | bytes 17301504 | tf_op jit(solution)/shard_map/reduce_scatter | solution.py:75
  18.4 28.4 %copy-start.7 = (s32[32]{0:T(128)S(1)}, s32[32]{0:T(128)}, u32[]{:S(2)}) copy-start(s32[32]{0:T(128)} %param.18) | copy-start | bytes 388
  18.4 28.4 %copy-start.2 = (bf16[1,8,32,576]{3,2,1,0:T(8,128)(2,1)S(1)}, bf16[1,8,32,576]{3,2,1,0:T(8,128)(2,1)}, u32[]{:S(2)}) copy-start(bf16[1,8,32,576]{3,2,1,0:T(8,128)(2,1)} %param.15) | copy-start | bytes 884740
  18.4 28.4 %copy-start.5 = (bf16[1,8,576]{2,1,0:T(8,128)(2,1)S(1)}, bf16[1,8,576]{2,1,0:T(8,128)(2,1)}, u32[]{:S(2)}) copy-start(bf16[1,8,576]{2,1,0:T(8,128)(2,1)} %param.16) | copy-start | bytes 27652
  230.9 2.2 copy-start.9
  233.0 141.2 %copy-start.6 = (s32[256,8]{0,1:T(8,128)S(1)}, s32[256,8]{0,1:T(8,128)}, u32[]{:S(2)}) copy-start(s32[256,8]{0,1:T(8,128)} %param.28) | copy-start | bytes 24580
  233.0 190.5 %copy-start.8 = (bf16[224]{0:T(256)(128)(2,1)S(1)}, bf16[224]{0:T(256)(128)(2,1)}, u32[]{:S(2)}) copy-start(bf16[224]{0:T(256)(128)(2,1)} %param.23) | copy-start | bytes 1348
  233.0 228.9 %copy-start.3 = (bf16[256,224]{0,1:T(8,128)(2,1)S(1)}, bf16[256,224]{0,1:T(8,128)(2,1)}, u32[]{:S(2)}) copy-start(bf16[256,224]{0,1:T(8,128)(2,1)} %param.22) | copy-start | bytes 344068
  233.0 186.8 %all-gather.6.cloned.1.call-start = ((), (), s32[]{:S(2)}) async-start(), calls=%async_computation.5 | async-start | bytes 2162688 | tf_op jit(solution)/shard_map/all_gather | solution.py:83
  374.1 87.8 %all-reduce.4.cloned.1.call-start = ((), (), s32[]{:S(2)}) async-start(), calls=%async_computation.6 | async-start | bytes 458752 | tf_op jit(solution)/shard_map/psum | solution.py:85
  423.4 199.7 %reduce-scatter.6.cloned.1.call-start = ((), (), s32[]{:S(2)}) async-start(), calls=%async_computation.7 | async-start | bytes 6488064 | tf_op jit(solution)/shard_map/reduce_scatter | solution.py:111
  461.9 333.6 %copy-start.1 = (f32[256,224]{0,1:T(8,128)S(1)}, f32[256,224]{0,1:T(8,128)}, u32[]{:S(2)}) copy-start(f32[256,224]{0,1:T(8,128)} %all-reduce.4.cloned.1.call-done) | copy-start | bytes 688132
  532.0 263.5 %copy-start.4 = (bf16[256,224]{0,1:T(8,128)(2,1)S(1)}, bf16[256,224]{0,1:T(8,128)(2,1)}, u32[]{:S(2)}) copy-start(bf16[256,224]{0,1:T(8,128)(2,1)} %param.22) | copy-start | bytes 344068
  540.3 162.6 %reduce-scatter.8.cloned.1.call-start = ((), (), s32[]{:S(2)}) async-start(), calls=%async_computation.9 | async-start | bytes 540672 | tf_op jit(solution)/shard_map/reduce_scatter | solution.py:114
  542.6 209.1 %all-gather.8.cloned.1.call-start = ((), (), s32[]{:S(2)}) async-start(), calls=%async_computation.8 | async-start | bytes 3244032 | tf_op jit(solution)/shard_map/all_gather | solution.py:121
  624.8 170.7 %all-reduce.6.cloned.1.call-start = ((), (), s32[]{:S(2)}) async-start(), calls=%async_computation.10 | async-start | bytes 229376 | tf_op jit(solution)/shard_map/psum | solution.py:132
Sparse Core Ops, SparseCore 0:
  9.6 61.5 all-gather.3
  233.1 115.8 reduce-scatter.3
  374.2 45.5 all-gather.5
  423.6 38.2 all-reduce.3
  540.5 82.6 reduce-scatter.5
  626.4 76.3 reduce-scatter.7
  705.2 46.4 all-gather.7
  758.2 37.2 all-reduce.5
where the time goes:
time: 807 us; the launch traced here: 804 us
  blocking collectives  339 us (42%)
  waiting for transfers between devices  305 us (38%)
  matrix products  65.9 us (8%)
  local copies, waits for them, and re-layouts  43.3 us (5%)
  other arithmetic  37.1 us (5%)
  between operations  13.7 us (2%)
    unnamed x1, blocking collectives  126 us
    pmax x1, blocking collectives, per_device(): row_top = lax.pmax(local_top, 'pre')  121 us
    reduce_scatter x1, waiting for transfers between devices, per_device(): lax.psum_scatter(gate_up.astype(jnp.bfloat16), 'pre', scatter_dimension=3...  80.5 us
    reduce_scatter x1, waiting for transfers between devices, per_device(): lax.psum_scatter(shared_pair.astype(jnp.bfloat16), 'pre', scatter_dimensi...  76.2 us
    psum x1, blocking collectives, per_device(): squares = lax.psum(jnp.sum(hidden * hidden, -1), 'pre')  65.1 us
    all_gather x1, waiting for transfers between devices, per_device(): head_out = lax.all_gather(own_heads, 'pre', axis=0, tiled=True)  43.9 us
    gather x2, local copies, waits for them, and re-layouts, per_device(): prefix_rows = jnp.take(prefix_latents, prefix_of, axis=0)  38.7 us
    psum x1, waiting for transfers between devices, per_device(): attention = lax.psum(attention, 'exp')  38.4 us
  transfers between devices with their start and end apart: 8, of which 7 were waited for; matrix products, arithmetic and copies ran while one was open for 9% of the time, Pallas kernels for 0%

commit v1 on v0

v1 whole, which is shorter than its diff:
```python
import functools
import math

import jax
import jax.numpy as jnp
from jax import lax
from jax.experimental import pallas as pl
from jax.experimental.pallas import tpu as pltpu
from jax.sharding import PartitionSpec as P

D = 7168
LAT = 512
ROPE = 64
HD = 128
DRAFT = 8
EXP_DEV = 3
CAP = 192
RING = 4
CHIPS = 16
HEADS = 32
ROWS = HEADS * DRAFT
MSG = ROWS + 16
PIECE = 656
ACT = 320
KEXP = (HD + ROPE) ** (-0.5) * math.log2(math.e)
BF = jnp.bfloat16
F32 = jnp.float32
VMEM_LIMIT = 56 * 1024 * 1024


def device_of(z, x, c):
    return (z * RING + x) * 2 + c


def pre_pairs(move):
    return [
        (device_of(z, x, c), device_of(*move(z, x, c)))
        for z in range(RING)
        for x in range(RING)
        for c in range(2)
    ]


CORE = pre_pairs(lambda z, x, c: (z, x, 1 - c))
X_BY = {d: pre_pairs(lambda z, x, c: (z, (x + d) % RING, c)) for d in (1, 2, 3)}
Z_BY = {d: pre_pairs(lambda z, x, c: ((z + d) % RING, x, c)) for d in (1, 2, 3)}
Y_BY = {d: [(e, (e + d) % RING) for e in range(RING)] for d in (1, 2, 3)}
SAME_CORE = [[chip * 2 + c for chip in range(CHIPS)] for c in range(2)]


def swap_core(value):
    return lax.ppermute(value, "pre", CORE)


def ring_gather(value, pairs):
    return [value] + [lax.ppermute(value, "pre", pairs[d]) for d in (1, 2, 3)]


def exp_sum(value):
    others = {d: lax.ppermute(value, "exp", Y_BY[d]).astype(F32) for d in (1, 2, 3)}
    return (value.astype(F32) + others[2]) + (others[1] + others[3])


def chip_exchange(value):
    return lax.all_to_all(value, "pre", 0, 0, axis_index_groups=SAME_CORE)


def dot(a, b, dims=((1,), (0,))):
    return lax.dot_general(a, b, (dims, ((), ())), preferred_element_type=F32)


def eye(n):
    return lax.broadcasted_iota(jnp.int32, (n, n), 0) == lax.broadcasted_iota(jnp.int32, (n, n), 1)


def column_to_rows(column):
    mask = eye(128)
    parts = [
        jnp.sum(jnp.where(mask, jnp.broadcast_to(column[b * 128 : (b + 1) * 128], (128, 128)), 0.0), 0, keepdims=True)
        for b in range(column.shape[0] // 128)
    ]
    return jnp.concatenate(parts, 0)


def three_terms(rows):
    high = rows.astype(BF).astype(F32)
    rest = rows - high
    mid = rest.astype(BF).astype(F32)
    return [high, mid, rest - mid]


def near_kernel(q_ref, k_ref, w_ref, out_ref, stat_ref, acc):
    keys = k_ref[...]
    scores = dot(q_ref[...], keys, ((1,), (1,)))
    draft = lax.broadcasted_iota(jnp.int32, scores.shape, 0) % DRAFT
    key = lax.broadcasted_iota(jnp.int32, scores.shape, 1)
    allowed = key <= draft
    top = jnp.max(jnp.where(allowed, scores, -jnp.inf), 1, keepdims=True)
    weight = jnp.where(allowed, jnp.exp2((scores - top) * KEXP), 0.0).astype(BF)
    total = jnp.sum(weight.astype(F32), 1, keepdims=True)
    acc[...] = dot(weight, keys[:, :LAT])
    stat_ref[...] = jnp.concatenate([column_to_rows(top), column_to_rows(total)], 0)
    for h in range(HEADS):
        rows = slice(h * DRAFT, (h + 1) * DRAFT)
        out_ref[rows, :] = dot(acc[rows, :].astype(BF), w_ref[h])


def far_kernel(prompt, place, q0_ref, q1_ref, la_ref, lb_ref, w_ref, out_ref, acc):
    i = pl.program_id(0)
    q = jnp.concatenate([q0_ref[0], q1_ref[0]], 0)
    la = la_ref[0]
    lb = lb_ref[0]
    sa = dot(q, la, ((1,), (1,)))
    sb = dot(q, lb, ((1,), (1,)))
    top = jnp.max(jnp.maximum(sa, sb), 1, keepdims=True)
    wa = jnp.exp2((sa - top) * KEXP).astype(BF)
    wb = jnp.exp2((sb - top) * KEXP).astype(BF)
    total = jnp.sum(wa.astype(F32) + wb.astype(F32), 1, keepdims=True)
    summed = dot(wa, la[:, :LAT]) + dot(wb, lb[:, :LAT])
    to = place[i]
    acc[:, to] = summed.reshape(HEADS, DRAFT, LAT)
    extra = three_terms(column_to_rows(top)) + three_terms(column_to_rows(total))
    out_ref[to, ROWS:MSG, :] = jnp.concatenate(extra + [jnp.zeros((4, 128), F32)], 0).astype(BF)

    @pl.when(i == CHIPS - 1)
    def _():
        for pair in range(HEADS // 2):
            both = [
                dot(acc[h].reshape(CHIPS * DRAFT, LAT).astype(BF), w_ref[h]).reshape(CHIPS, DRAFT, HD)
                for h in (2 * pair, 2 * pair + 1)
            ]
            out_ref[:, pair * 16 : (pair + 1) * 16, :] = jnp.concatenate(both, 1).astype(BF)


def combine_kernel(rec_ref, near_ref, stat_ref, out_ref):
    tops, totals = [], []
    for p in range(CHIPS):
        extra = rec_ref[p, ROWS:MSG, :].astype(F32)
        tops.append(extra[0:2] + extra[2:4] + extra[4:6])
        totals.append(extra[6:8] + extra[8:10] + extra[10:12])
    tops.append(stat_ref[0:2])
    totals.append(stat_ref[2:4])
    best = functools.reduce(jnp.maximum, tops)
    scale = [jnp.exp2((t - best) * KEXP) for t in tops]
    whole = functools.reduce(jnp.add, [s * t for s, t in zip(scale, totals)])
    scale = [s / whole for s in scale]
    blocks = []
    for b in range(2):
        table = jnp.concatenate(
            [s[b : b + 1] for s in scale] + [jnp.zeros((128 - len(scale), 128), F32)], 0
        ).T
        rows = slice(b * 128, (b + 1) * 128)
        value = near_ref[rows, :] * table[:, CHIPS : CHIPS + 1]
        for p in range(CHIPS):
            value = value + rec_ref[p, rows, :].astype(F32) * table[:, p : p + 1]
        blocks.append(value)
    value = jnp.concatenate(blocks, 0)
    flat = jnp.concatenate([value[h * DRAFT : (h + 1) * DRAFT] for h in range(HEADS)], 1).astype(BF)
    for p in range(CHIPS):
        out_ref[p] = flat


def interleave(core, own, other):
    n, width = own.shape
    own = own.reshape(CHIPS, 1, DRAFT, width)
    other = other.reshape(CHIPS, 1, DRAFT, width)
    first = jnp.where(core == 0, own, other)
    second = jnp.where(core == 0, other, own)
    return jnp.concatenate([first, second], 1).reshape(2 * n, width)


def gate_up_kernel(
    core_ref, own_ref, rcv_ref, gm_ref, go_ref, pick_ref, wm_ref, wo_ref, sm_ref, so_ref, out_ref, xm, xo
):
    e = pl.program_id(0)
    core = core_ref[0]

    @pl.when(e == 0)
    def _():
        hm = interleave(core, own_ref[0], rcv_ref[1])
        ho = interleave(core, own_ref[1], rcv_ref[0])
        square = jnp.sum(hm * hm, 1, keepdims=True) + jnp.sum(ho * ho, 1, keepdims=True)
        terms = three_terms(column_to_rows(square))
        rows = jnp.concatenate(terms + [jnp.zeros((10, 128), F32)], 0).astype(BF)
        xm[...] = (hm * gm_ref[...].astype(F32)).astype(BF)
        xo[...] = (ho * go_ref[...].astype(F32)).astype(BF)
        for i in range(CHIPS):
            out_ref[i, 640:656, :] = rows
        for g in range(2):
            pair = (dot(xm[...], sm_ref[g]) + dot(xo[...], so_ref[g])).astype(BF)
            for i in range(CHIPS):
                out_ref[i, 576 + g * 32 : 608 + g * 32, :] = pair[
                    (i % 8) * 32 : (i % 8 + 1) * 32, (i // 8) * 128 : (i // 8 + 1) * 128
                ]

    picked_m = dot(pick_ref[0], xm[...]).astype(BF)
    picked_o = dot(pick_ref[0], xo[...]).astype(BF)
    for g in range(2):
        pair = (dot(picked_m, wm_ref[g, 0]) + dot(picked_o, wo_ref[g, 0])).astype(BF)
        start = pl.multiple_of(g * 288 + e * 96, 16)
        for i in range(CHIPS):
            out_ref[i, pl.ds(start, 96), :] = pair[
                (i % 2) * 96 : (i % 2 + 1) * 96, (i // 2) * 128 : (i // 2 + 1) * 128
            ]


def act_kernel(rec_ref, pick_ref, out_ref, acc):
    i = pl.program_id(0)
    part = rec_ref[0].astype(F32)
    for p in range(1, 4):
        part = part + rec_ref[p].astype(F32)

    @pl.when(i == 0)
    def _():
        acc[...] = part

    @pl.when(i > 0)
    def _():
        acc[...] += part

    @pl.when(i == 3)
    def _():
        square = acc[640:642, :] + acc[642:644, :] + acc[644:646, :]
        inverse = lax.rsqrt(square / D + 1e-06)
        pick = pick_ref[...].astype(F32)
        factor = jnp.sum(pick[:, :128] * inverse[0:1] + pick[:, 128:] * inverse[1:2], 1, keepdims=True)
        gate = jnp.concatenate([acc[0:288, :], acc[576:608, :]], 0) * factor
        up = jnp.concatenate([acc[288:576, :], acc[608:640, :]], 0) * factor
        act = (jax.nn.silu(gate) * up).astype(BF)
        for p in range(CHIPS):
            out_ref[p] = act


def down_kernel(act_ref, wm_ref, wo_ref, sm_ref, so_ref, weight_ref, spread_ref, mine_ref, other_ref):
    pieces = []
    for e in range(EXP_DEV):
        rows = slice(e * 96, (e + 1) * 96)
        pieces.append(
            jnp.concatenate(
                [jnp.concatenate([act_ref[u * 2 + half, rows, :] for u in range(8)], 1) for half in range(2)], 0
            )
        )
    shared = jnp.concatenate(
        [jnp.concatenate([act_ref[u * 8 + t, 288:320, :] for u in range(2)], 1) for t in range(8)], 0
    )
    for w_ref, s_ref, out_ref in ((wm_ref, sm_ref, mine_ref), (wo_ref, so_ref, other_ref)):
        weighted = jnp.concatenate(
            [
                (dot(pieces[e], w_ref[e]) * weight_ref[e * CAP : (e + 1) * CAP, :]).astype(BF)
                for e in range(EXP_DEV)
            ],
            0,
        )
        total = dot(spread_ref[...], weighted) + dot(shared, s_ref[...])
        out_ref[...] = total.astype(out_ref.dtype)


def params(n=0):
    if n:
        return pltpu.CompilerParams(vmem_limit_bytes=VMEM_LIMIT, dimension_semantics=("arbitrary",) * n)
    return pltpu.CompilerParams(vmem_limit_bytes=VMEM_LIMIT)


def near_part(q, keys, w_uv):
    return pl.pallas_call(
        near_kernel,
        out_shape=(jax.ShapeDtypeStruct((ROWS, HD), F32), jax.ShapeDtypeStruct((4, 128), F32)),
        scratch_shapes=[pltpu.VMEM((ROWS, LAT), F32)],
        compiler_params=params(),
        name="near",
    )(q, keys, w_uv)


def far_part(prompt, place, q0, q1, la, lb, w_uv):
    width = LAT + ROPE
    positions = la.shape[1]
    latent = pl.BlockSpec((1, positions, width), lambda i, pr, to: (pr[i], 0, 0))
    return pl.pallas_call(
        far_kernel,
        out_shape=jax.ShapeDtypeStruct((CHIPS, MSG, HD), BF),
        grid_spec=pltpu.PrefetchScalarGridSpec(
            num_scalar_prefetch=2,
            grid=(CHIPS,),
            in_specs=[
                pl.BlockSpec((1, ROWS // 2, width), lambda i, pr, to: (i, 0, 0)),
                pl.BlockSpec((1, ROWS // 2, width), lambda i, pr, to: ((i % RING) * RING + i // RING, 0, 0)),
                latent,
                latent,
                pl.BlockSpec((HEADS, LAT, HD), lambda i, pr, to: (0, 0, 0)),
            ],
            out_specs=pl.BlockSpec((CHIPS, MSG, HD), lambda i, pr, to: (0, 0, 0)),
            scratch_shapes=[pltpu.VMEM((HEADS, CHIPS, DRAFT, LAT), F32)],
        ),
        compiler_params=params(1),
        name="far",
    )(prompt, place, q0, q1, la, lb, w_uv)


def combine(received, near_out, near_stat):
    return pl.pallas_call(
        combine_kernel,
        out_shape=jax.ShapeDtypeStruct((CHIPS, DRAFT, HEADS * HD), BF),
        compiler_params=params(),
        name="combine",
    )(received, near_out, near_stat)


def gate_up(core, own, rcv, gain_m, gain_o, pick, wm, wo, sm, so):
    width = own.shape[-1]
    half = wm.shape[-1]

    def whole(*shape):
        return pl.BlockSpec(shape, lambda e, c: (0,) * len(shape))

    weights = pl.BlockSpec((2, 1, width, half), lambda e, c: (0, e, 0, 0))
    return pl.pallas_call(
        gate_up_kernel,
        out_shape=jax.ShapeDtypeStruct((CHIPS, PIECE, 128), BF),
        grid_spec=pltpu.PrefetchScalarGridSpec(
            num_scalar_prefetch=1,
            grid=(EXP_DEV,),
            in_specs=[
                whole(*own.shape),
                whole(*rcv.shape),
                whole(1, width),
                whole(1, width),
                pl.BlockSpec((1, CAP, 256), lambda e, c: (e, 0, 0)),
                weights,
                weights,
                whole(*sm.shape),
                whole(*so.shape),
            ],
            out_specs=whole(CHIPS, PIECE, 128),
            scratch_shapes=[pltpu.VMEM((256, width), BF), pltpu.VMEM((256, width), BF)],
        ),
        compiler_params=params(1),
        name="gate_up",
    )(core, own, rcv, gain_m, gain_o, pick, wm, wo, sm, so)


def activate(received, pick):
    return pl.pallas_call(
        act_kernel,
        out_shape=jax.ShapeDtypeStruct((CHIPS, ACT, 128), BF),
        grid=(4,),
        in_specs=[
            pl.BlockSpec((4, PIECE, 128), lambda i: (i, 0, 0)),
            pl.BlockSpec((ACT, 256), lambda i: (0, 0)),
        ],
        out_specs=pl.BlockSpec((CHIPS, ACT, 128), lambda i: (0, 0, 0)),
        scratch_shapes=[pltpu.VMEM((PIECE, 128), F32)],
        compiler_params=params(1),
        name="activate",
    )(received, pick)


def down(acts, wm, wo, sm, so, weight, spread):
    width = wm.shape[-1]
    return pl.pallas_call(
        down_kernel,
        out_shape=(jax.ShapeDtypeStruct((256, width), F32), jax.ShapeDtypeStruct((256, width), BF)),
        compiler_params=params(),
        name="down",
    )(acts, wm, wo, sm, so, weight, spread)


def halves(value, core, axis):
    size = value.shape[axis] // 2
    mine = lax.dynamic_slice_in_dim(value, core * size, size, axis)
    other = lax.dynamic_slice_in_dim(value, (1 - core) * size, size, axis)
    return mine, other


def per_device(
    queries,
    draft_latents,
    prefix_latents,
    prefix_of,
    accepted,
    w_uv,
    w_out,
    residual,
    norm_gain,
    w_gate_up,
    w_down,
    shared_gate_up,
    shared_down,
    expert_ids,
    expert_gates,
):
    pre = lax.axis_index("pre")
    core, chip = pre % 2, pre // 2
    z, x = chip // RING, chip % RING
    tokens = expert_ids.shape[0]

    q_own = queries[0].transpose(1, 0, 2).reshape(ROWS, LAT + ROPE)
    first = jnp.stack(ring_gather(q_own[: ROWS // 2], X_BY))
    second = jnp.stack(ring_gather(q_own[ROWS // 2 :], Z_BY))
    q0 = jnp.concatenate(ring_gather(first, Z_BY))
    q1 = jnp.concatenate(ring_gather(second, X_BY))

    latents_other = swap_core(prefix_latents)
    w_out_other = swap_core(w_out)
    residual_other = swap_core(residual)
    gain_other = swap_core(norm_gain)
    pair_m, pair_send = halves(w_gate_up.transpose(2, 0, 1, 3), core, 3)
    pair_o = swap_core(pair_send)
    shared_m, shared_send = halves(shared_gate_up.transpose(1, 0, 2), core, 2)
    shared_o = swap_core(shared_send)
    down_m, down_send = halves(w_down, core, 1)
    down_o = swap_core(down_send)
    shared_down_m, shared_down_send = halves(shared_down, core, 0)
    shared_down_o = swap_core(shared_down_send)

    live = (jnp.arange(DRAFT)[None, :] < accepted[:, None]).reshape(tokens).astype(F32)
    local_experts = lax.axis_index("exp") * EXP_DEV + jnp.arange(EXP_DEV, dtype=jnp.int32)
    chosen = expert_ids[:, :, None] == local_experts[None, None, :]
    routed = jnp.any(chosen, 1)
    weights = jnp.sum(jnp.where(chosen, expert_gates[:, :, None], 0.0), 1) * live[:, None]
    position = jnp.cumsum(routed.astype(jnp.int32), 0) - 1
    slot_hit = routed.T[:, None, :] & (
        position.T[:, None, :] == jnp.arange(CAP, dtype=jnp.int32)[None, :, None]
    )
    pick = slot_hit.astype(BF)
    spread = slot_hit.reshape(EXP_DEV * CAP, tokens).T.astype(BF)
    slot_weight = jnp.sum(jnp.where(slot_hit, weights.T[:, None, :], 0.0), 2).reshape(EXP_DEV * CAP, 1)
    my_slots = lax.dynamic_slice_in_dim(pick, (chip % 2) * 96, 96, 1).reshape(288, tokens)
    my_tokens = (
        jnp.arange(tokens, dtype=jnp.int32)[None, :]
        == (chip % 8) * 32 + jnp.arange(32, dtype=jnp.int32)[:, None]
    ).astype(BF)
    my_pick = jnp.concatenate([my_slots, my_tokens], 0)

    near_keys = jnp.pad(draft_latents[0], ((0, 128 - DRAFT), (0, 0)))
    near_out, near_stat = near_part(q_own, near_keys, w_uv)

    step = jnp.arange(CHIPS, dtype=jnp.int32)
    place = ((z - step // RING) % RING) * RING + (x - step % RING) % RING
    prompt = jnp.take(prefix_of, place * 2 + core, axis=0)
    messages = far_part(prompt, place, q0, q1, prefix_latents, latents_other, w_uv)
    heads = combine(chip_exchange(messages), near_out, near_stat)
    head_out = chip_exchange(heads).reshape(CHIPS * DRAFT, HEADS * HD)

    attention = jnp.stack([dot(head_out, w_out), dot(head_out, w_out_other)]).astype(BF)

    def own_tokens(value):
        value = value.reshape(CHIPS, 2, DRAFT, value.shape[-1])
        return lax.dynamic_index_in_dim(value, core, 1, False).reshape(CHIPS * DRAFT, -1)

    skip = jnp.stack([own_tokens(residual), own_tokens(residual_other)]).astype(F32)
    hidden = skip + exp_sum(attention)
    hidden_rcv = swap_core(hidden)

    pieces = gate_up(
        core[None].astype(jnp.int32),
        hidden,
        hidden_rcv,
        norm_gain[None],
        gain_other[None],
        pick,
        pair_m,
        pair_o,
        shared_m,
        shared_o,
    )
    acts = activate(chip_exchange(pieces), my_pick)
    mine, other = down(
        chip_exchange(acts), down_m, down_o, shared_down_m, shared_down_o, slot_weight, spread
    )
    mixed = exp_sum((mine + swap_core(other).astype(F32)).astype(BF))
    return (interleave(core, hidden[0], hidden_rcv[1]) + mixed).astype(BF)


def solution(mesh):
    return jax.shard_map(
        per_device,
        mesh=mesh,
        in_specs=(
            P("pre", None, "exp", None),
            P("pre", None, None),
            P(None, "pre", None),
            P(),
            P(),
            P("exp", None, None),
            P("exp", "pre"),
            P(None, "pre"),
            P("pre"),
            P("exp", "pre", None, None),
            P("exp", None, "pre"),
            P("pre", None, "exp"),
            P("exp", "pre"),
            P(),
            P(),
        ),
        out_specs=P(None, "pre"),
        check_vma=False,
    )
```

time: 807 us -> 293 us (0.36)
  blocking collectives: 339 us -> 0 us
  waiting for transfers between devices: 305 us -> 90.5 us
  starting transfers between devices: 0.29 us -> 61.4 us
  matrix products: 65.9 us -> 5.18 us
  Pallas kernels: 0 us -> 49 us
  local copies, waits for them, and re-layouts: 43.3 us -> 76.2 us
  other arithmetic: 37.1 us -> 8.27 us
  between operations: 13.7 us -> 0.44 us
    reduce_scatter x3 -> x0, waiting for transfers between devices: 157 us -> none  [the longest x1 80.5 us: per_device(): lax.psum_scatter(gate_up.astype(jnp.bfloat16), 'pre', scatter_dimension=3...]
    unnamed x1 -> x0, blocking collectives: 126 us -> none
    pmax x1 -> x0, blocking collectives: 121 us -> none  [per_device(): row_top = lax.pmax(local_top, 'pre')]
    psum x2 -> x0, waiting for transfers between devices: 75.7 us -> none  [the longest x1 38.4 us: per_device(): attention = lax.psum(attention, 'exp')]
    all_gather x3 -> x0, waiting for transfers between devices: 71.8 us -> none  [the longest x1 43.9 us: per_device(): head_out = lax.all_gather(own_heads, 'pre', axis=0, tiled=True)]
    psum x1 -> x0, blocking collectives: 65.1 us -> none  [per_device(): squares = lax.psum(jnp.sum(hidden * hidden, -1), 'pre')]
    dot_general x11 -> x2, matrix products: 65.9 us -> 5.18 us  [dot(): return lax.dot_general(a, b, (dims, ((), ())), preferred_element_type=F32)]
    all_to_all x0 -> x4, waiting for transfers between devices: none -> 59.7 us  [chip_exchange(): return lax.all_to_all(value, 'pre', 0, 0, axis_index_groups=SAME_CORE)]
  transfers between devices with their start and end apart: 8 -> 32, of which waited for: 7 -> 10; matrix products, arithmetic and copies ran while one was open for 9% -> 26% of each run, Pallas kernels for 0% -> 4%
where the time goes in v1:
time: 293 us; the launch traced here: 291 us
  waiting for transfers between devices  90.5 us (31%)
  local copies, waits for them, and re-layouts  76.2 us (26%)
  starting transfers between devices  61.4 us (21%)
  Pallas kernels  49 us (17%)
  other arithmetic  8.27 us (3%)
  matrix products  5.18 us (2%)
    all_to_all x4, waiting for transfers between devices, chip_exchange(): return lax.all_to_all(value, 'pre', 0, 0, axis_index_groups=SAME_CORE)  59.7 us
    unnamed x75, local copies, waits for them, and re-layouts  29.8 us
    pallas_call x1, Pallas kernels, far_part(): pl.pallas_call(far_kernel, out_shape=jax.ShapeDtypeStruct((CHIPS, MSG, HD...  26.3 us
    ppermute x12, waiting for transfers between devices, ring_gather(): return [value] + [lax.ppermute(value, 'pre', pairs[d]) for d in (1, 2, 3)]  23.5 us
    all_to_all x4, starting transfers between devices, chip_exchange(): return lax.all_to_all(value, 'pre', 0, 0, axis_index_groups=SAME_CORE)  19.1 us
    ppermute x10, starting transfers between devices, swap_core(): return lax.ppermute(value, 'pre', CORE)  18.3 us
    ppermute x12, starting transfers between devices, ring_gather(): return [value] + [lax.ppermute(value, 'pre', pairs[d]) for d in (1, 2, 3)]  14.6 us
    ppermute x6, local copies, waits for them, and re-layouts, ring_gather(): return [value] + [lax.ppermute(value, 'pre', pairs[d]) for d in (1, 2, 3)]  12.3 us
  transfers between devices with their start and end apart: 32, of which 10 were waited for; matrix products, arithmetic and copies ran while one was open for 26% of the time, Pallas kernels for 4%

profile of v1, /device:TPU:1, one launch (start us, length us, event | category | flops | bytes accessed | tf_op | source)
XLA Modules:
  0.0 290.9 jit_solution(15577081437957678877)
XLA Ops:
  4.9 3.3 %collective-permute-start.8 = (bf16[128,576]{1,0:T(8,128)(2,1)}, bf16[128,576]{1,0:T(8,128)(2,1)S(1)}, u32[]{:S(2)}, u32[]{:S(2)}) collective-permute-start(bf16[128,576]{1,0:T(8,128)(2,1)} %bitcast.59.clone.2), channel_id=1, source_target_pairs={{0,64},{4,68},{8,72},{12,76},{16,80},{20,84},{24,88},{28,92},{32,9... | collective-permute-start | bytes 442376 | tf_op jit(solution)/shard_map/ppermute | solution.py:56
  19.3 7.7 %copy.171.la_ref = bf16[8,512,576]{2,1,0:T(8,128)(2,1)} copy(bf16[8,512,576]{1,2,0:T(8,128)(2,1)} %param.17) | data formatting | bytes 9437184 | tf_op args[2]
  39.3 6.3 %collective-permute-done.10 = bf16[4,128,576]{1,2,0:T(8,128)(2,1)} collective-permute-done((bf16[4,128,576]{1,2,0:T(8,128)(2,1)}, bf16[4,128,576]{1,2,0:T(8,128)(2,1)}, u32[]{:S(2)}, u32[]{:S(2)}) %collective-permute-start.10) | collective-permute-done | bytes 589856 | tf_op jit(solution)/shard_map/ppermute | solution.py:56
  45.6 10.8 %collective-permute-done.11 = bf16[4,128,576]{1,2,0:T(8,128)(2,1)} collective-permute-done((bf16[4,128,576]{1,2,0:T(8,128)(2,1)}, bf16[4,128,576]{1,2,0:T(8,128)(2,1)}, u32[]{:S(2)}, u32[]{:S(2)}) %collective-permute-start.11) | collective-permute-done | bytes 589856 | tf_op jit(solution)/shard_map/ppermute | solution.py:56
  68.3 4.9 %collective-permute-done.6 = bf16[4,128,576]{1,2,0:T(8,128)(2,1)} collective-permute-done((bf16[4,128,576]{1,2,0:T(8,128)(2,1)}, bf16[4,128,576]{1,2,0:T(8,128)(2,1)}, u32[]{:S(2)}, u32[]{:S(2)}) %collective-permute-start.6) | collective-permute-done | bytes 589856 | tf_op jit(solution)/shard_map/ppermute | solution.py:56
  79.7 8.1 %copy.172.lb_ref = bf16[8,512,576]{2,1,0:T(8,128)(2,1)} copy(bf16[8,512,576]{1,2,0:T(8,128)(2,1)} %collective-permute-done.13) | data formatting | bytes 9437184 | tf_op jit(solution)/shard_map/ppermute | solution.py:52
  87.8 26.3 %far.1 = bf16[16,272,128]{2,1,0:T(8,128)(2,1)} custom-call(s32[16]{0:T(128)} %get-tuple-element.13.prompt, s32[16]{0:T(128)} %get-tuple-element.14.place, bf16[16,128,576]{2,1,0:T(8,128)(2,1)} %copy-done.5, bf16[16,128,576]{2,1,0:T(8,128)(2,1)} %constant_dynamic-update-slice_fusion.7.q1_ref, bf16[8,512,576]{2,1,0:T(8,128)(2,1)} %copy.171.la_ref, ...), custom_call_target="tpu_custom_call" | custom-call | tf_op jit(solution)/shard_map/far/pallas_call | solution.py:278
  114.1 4.7 %all-to-all-start = ((bf16[16,272,128]{2,1,0:T(8,128)(2,1)}), bf16[16,272,128]{2,1,0:T(8,128)(2,1)}, u32[]{:S(2)}, u32[]{:S(2)}) async-start(bf16[16,272,128]{2,1,0:T(8,128)(2,1)} %far.1), calls=%async_computation | async-start | bytes 2228224 | tf_op jit(solution)/shard_map/all_to_all | solution.py:65
  118.8 5.4 %collective-permute-start.14 = (bf16[4096,224]{0,1:T(8,128)(2,1)}, bf16[4096,224]{0,1:T(8,128)(2,1)}, u32[]{:S(2)}, u32[]{:S(2)}) collective-permute-start(bf16[4096,224]{0,1:T(8,128)(2,1)} %param.21), channel_id=1, source_target_pairs={{0,4},{4,0},{8,12},{12,8},{16,20},{20,16},{24,28},{28,24},{32,36},... | collective-permute-start | bytes 5505032 | tf_op jit(solution)/shard_map/ppermute | solution.py:52
  124.2 6.4 %constant_dynamic-slice_fusion.7 = (bf16[3,224,2,1024]{3,2,1,0:T(2,128)(2,1)S(1)}, bf16[3,224,2,1024]{3,2,1,0:T(2,128)(2,1)S(1)}) fusion(bf16[3,224,2,2048]{3,2,1,0:T(2,128)(2,1)} %param.24, s32[]{:T(128)S(6)} %select_n.196, s32[]{:T(128)S(6)} %select_n.195), kind=kLoop, calls=%fused_computation.69 | loop fusion | bytes 11010056 | tf_op jit(solution)/shard_map/dynamic-slice.1
  134.5 4.2 %near.1 = (f32[256,128]{1,0:T(8,128)}, f32[4,128]{1,0:T(4,128)}) custom-call(bf16[256,576]{1,0:T(8,128)(2,1)} %bitcast.94, bf16[128,576]{1,0:T(8,128)(2,1)} %pad.4.k_ref, bf16[32,512,128]{2,1,0:T(8,128)(2,1)} %w_ref.3), custom_call_target="tpu_custom_call" | custom-call | tf_op jit(solution)/shard_map/near/pallas_call | solution.py:265
  138.7 3.4 %combine.1 = bf16[16,8,4096]{2,1,0:T(8,128)(2,1)} custom-call(bf16[16,272,128]{2,1,0:T(8,128)(2,1)} %all-to-all-done.rec_ref, f32[256,128]{1,0:T(8,128)} %get-tuple-element.9.near_ref, f32[4,128]{1,0:T(4,128)} %get-tuple-element.10.stat_ref), custom_call_target="tpu_custom_call" | custom-call | tf_op jit(solution)/shard_map/combine/pallas_call | solution.py:300
  142.1 6.6 %all-to-all-start.1 = ((bf16[16,8,4096]{2,1,0:T(8,128)(2,1)}), bf16[16,8,4096]{2,1,0:T(8,128)(2,1)}, u32[]{:S(2)}, u32[]{:S(2)}) async-start(bf16[16,8,4096]{2,1,0:T(8,128)(2,1)} %combine.1), calls=%async_computation.1 | async-start | bytes 2097152 | tf_op jit(solution)/shard_map/all_to_all | solution.py:65
  152.5 12.5 %all-to-all-done.1 = bf16[16,8,4096]{2,1,0:T(8,128)(2,1)} async-done(((bf16[16,8,4096]{2,1,0:T(8,128)(2,1)}), bf16[16,8,4096]{2,1,0:T(8,128)(2,1)}, u32[]{:S(2)}, u32[]{:S(2)}) %all-to-all-start.1) | async-done | bytes 1048608 | tf_op jit(solution)/shard_map/all_to_all | solution.py:65
  165.0 2.6 fusion
  167.6 2.6 fusion.1
  170.2 3.0 %collective-permute-start.15 = (bf16[2,128,224]{2,1,0:T(8,128)(2,1)S(1)}, bf16[2,128,224]{2,1,0:T(8,128)(2,1)S(1)}, u32[]{:S(2)}, u32[]{:S(2)}) collective-permute-start(bf16[2,128,224]{2,1,0:T(8,128)(2,1)S(1)} %pad_maximum_fusion.4), channel_id=1, source_target_pairs={{0,2},{1,3},{2,0},{3,1},{4,6},{5,7},{6,4},{7,5},{8,10},{9,11},{10,... | collective-permute-start | bytes 344072 | tf_op jit(solution)/shard_map/ppermute | solution.py:60
  176.0 3.3 %collective-permute-start.21 = (bf16[2,224,256]{2,1,0:T(8,128)(2,1)S(1)}, bf16[2,224,256]{2,1,0:T(8,128)(2,1)S(1)}, u32[]{:S(2)}, u32[]{:S(2)}) collective-permute-start(bf16[2,224,256]{2,1,0:T(8,128)(2,1)S(1)} %bitcast.104), channel_id=1, source_target_pairs={{0,4},{4,0},{8,12},{12,8},{16,20},{20,16},{24,28},{28,24},{32,36},... | collective-permute-start | bytes 688136 | tf_op jit(solution)/shard_map/ppermute | solution.py:52
  179.8 2.6 collective-permute-start.18
  188.4 6.6 %gate_up.1 = bf16[16,656,128]{2,1,0:T(8,128)(2,1)} custom-call(s32[1]{0:T(128)} %bitcast.28.core_ref, f32[2,128,224]{2,1,0:T(8,128)} %copy-done.11, f32[2,128,224]{2,1,0:T(8,128)} %copy-done.16, bf16[1,224]{1,0:T(2,128)(2,1)} %broadcast_in_dim.48.gm_ref, bf16[1,224]{1,0:T(2,128)(2,1)} %broadcast_in_dim.49.go_ref, bf16[3,192,256]{2,1,0:T(8,128)(2,1)} %fusion.5.pick_ref, ...), custom_call_target="tpu_custom_call" | custom-call | tf_op jit(solution)/shard_map/gate_up/pallas_call | solution.py:316
  195.0 3.7 %all-to-all-start.2 = ((bf16[16,656,128]{2,1,0:T(8,128)(2,1)}), bf16[16,656,128]{2,1,0:T(8,128)(2,1)S(1)}, u32[]{:S(2)}, u32[]{:S(2)}) async-start(bf16[16,656,128]{2,1,0:T(8,128)(2,1)} %gate_up.1), calls=%async_computation.2 | async-start | bytes 5373952 | tf_op jit(solution)/shard_map/all_to_all | solution.py:65
  198.7 3.9 %constant_dynamic-slice_fusion.2 = (bf16[3,1024,224]{1,2,0:T(8,128)(2,1)}, bf16[3,1024,224]{1,2,0:T(8,128)(2,1)}) fusion(bf16[3,2048,224]{1,2,0:T(8,128)(2,1)} %param.25, s32[]{:T(128)S(6)} %select_n.196, s32[]{:T(128)S(6)} %select_n.195), kind=kLoop, calls=%fused_computation.64 | loop fusion | bytes 5505032 | tf_op jit(solution)/shard_map/dynamic_slice | solution.py:370
  203.4 37.8 %all-to-all-done.2.rec_ref = bf16[16,656,128]{2,1,0:T(8,128)(2,1)S(1)} async-done(((bf16[16,656,128]{2,1,0:T(8,128)(2,1)}), bf16[16,656,128]{2,1,0:T(8,128)(2,1)S(1)}, u32[]{:S(2)}, u32[]{:S(2)}) %all-to-all-start.2) | async-done | bytes 2687008 | tf_op jit(solution)/shard_map/all_to_all | solution.py:65
  242.7 4.1 %activate.1 = bf16[16,320,128]{2,1,0:T(8,128)(2,1)} custom-call(bf16[16,656,128]{2,1,0:T(8,128)(2,1)} %copy-done.2, bf16[320,256]{1,0:T(8,128)(2,1)} %pad_maximum_fusion.3.pick_ref), custom_call_target="tpu_custom_call" | custom-call | tf_op jit(solution)/shard_map/activate/pallas_call | solution.py:342
  246.8 4.1 %all-to-all-start.3 = ((bf16[16,320,128]{2,1,0:T(8,128)(2,1)}), bf16[16,320,128]{2,1,0:T(8,128)(2,1)S(1)}, u32[]{:S(2)}, u32[]{:S(2)}) async-start(bf16[16,320,128]{2,1,0:T(8,128)(2,1)} %activate.1), calls=%async_computation.3 | async-start | bytes 2621440 | tf_op jit(solution)/shard_map/all_to_all | solution.py:65
  257.5 2.5 copy.190.wo_ref
  260.1 9.3 %all-to-all-done.3.act_ref = bf16[16,320,128]{2,1,0:T(8,128)(2,1)S(1)} async-done(((bf16[16,320,128]{2,1,0:T(8,128)(2,1)}), bf16[16,320,128]{2,1,0:T(8,128)(2,1)S(1)}, u32[]{:S(2)}, u32[]{:S(2)}) %all-to-all-start.3) | async-done | bytes 1310752 | tf_op jit(solution)/shard_map/all_to_all | solution.py:65
  270.5 4.5 %down.1 = (f32[256,224]{1,0:T(8,128)}, bf16[256,224]{1,0:T(8,128)(2,1)}) custom-call(bf16[16,320,128]{2,1,0:T(8,128)(2,1)} %copy-done.4, bf16[3,1024,224]{2,1,0:T(8,128)(2,1)} %copy.199.wm_ref, bf16[3,1024,224]{2,1,0:T(8,128)(2,1)} %copy.190.wo_ref, bf16[256,224]{1,0:T(8,128)(2,1)} %copy.200.sm_ref, bf16[256,224]{1,0:T(8,128)(2,1)} %copy-done.20, ...), custom_call_target="tpu_custom_call" | custom-call | tf_op jit(solution)/shard_map/down/pallas_call | solution.py:359
  275.0 3.1 %collective-permute-start.24 = (bf16[256,224]{1,0:T(8,128)(2,1)}, bf16[256,224]{1,0:T(8,128)(2,1)S(1)}, u32[]{:S(2)}, u32[]{:S(2)}) collective-permute-start(bf16[256,224]{1,0:T(8,128)(2,1)} %get-tuple-element.12), channel_id=1, source_target_pairs={{0,4},{4,0},{8,12},{12,8},{16,20},{20,16},{24,28},{28,24},{32,36},... | collective-permute-start | bytes 344072 | tf_op jit(solution)/shard_map/ppermute | solution.py:52
  281.0 2.9 %collective-permute-start.26 = (bf16[256,224]{1,0:T(8,128)(2,1)S(1)}, bf16[256,224]{1,0:T(8,128)(2,1)S(1)}, u32[]{:S(2)}, u32[]{:S(2)}) collective-permute-start(bf16[256,224]{1,0:T(8,128)(2,1)S(1)} %add_convert_fusion), channel_id=1, source_target_pairs={{0,1},{1,2},{2,3},{3,0},{4,5},{5,6},{6,7},{7,4},{8,9},{9,10},{10,1... | collective-permute-start | bytes 344072 | tf_op jit(solution)/shard_map/ppermute | solution.py:60
  283.9 2.6 collective-permute-done.25
  286.6 3.5 %collective-permute-done.26 = bf16[256,224]{1,0:T(8,128)(2,1)S(1)} collective-permute-done((bf16[256,224]{1,0:T(8,128)(2,1)S(1)}, bf16[256,224]{1,0:T(8,128)(2,1)S(1)}, u32[]{:S(2)}, u32[]{:S(2)}) %collective-permute-start.26) | collective-permute-done | bytes 114720 | tf_op jit(solution)/shard_map/ppermute | solution.py:60
  (182 shorter events, 77.4 us)
Async XLA Ops:
  0.0 79.7 %collective-permute-start.13 = (bf16[8,512,576]{1,2,0:T(8,128)(2,1)}, bf16[8,512,576]{1,2,0:T(8,128)(2,1)}, u32[]{:S(2)}, u32[]{:S(2)}) collective-permute-start(bf16[8,512,576]{1,2,0:T(8,128)(2,1)} %param.17), channel_id=1, source_target_pairs={{0,4},{4,0},{8,12},{12,8},{16,20},{20,16},{24,28},{28,24},{32,36},... | collective-permute-start | bytes 14155784 | tf_op jit(solution)/shard_map/ppermute | solution.py:52
  3.2 9.1 %collective-permute-start.7 = (bf16[128,576]{1,0:T(8,128)(2,1)}, bf16[128,576]{1,0:T(8,128)(2,1)S(1)}, u32[]{:S(2)}, u32[]{:S(2)}) collective-permute-start(bf16[128,576]{1,0:T(8,128)(2,1)} %bitcast.59.clone.2), channel_id=1, source_target_pairs={{0,32},{4,36},{8,40},{12,44},{16,48},{20,52},{24,56},{28,60},{32,6... | collective-permute-start | bytes 442376 | tf_op jit(solution)/shard_map/ppermute | solution.py:56
  4.9 11.4 %collective-permute-start.8 = (bf16[128,576]{1,0:T(8,128)(2,1)}, bf16[128,576]{1,0:T(8,128)(2,1)S(1)}, u32[]{:S(2)}, u32[]{:S(2)}) collective-permute-start(bf16[128,576]{1,0:T(8,128)(2,1)} %bitcast.59.clone.2), channel_id=1, source_target_pairs={{0,64},{4,68},{8,72},{12,76},{16,80},{20,84},{24,88},{28,92},{32,9... | collective-permute-start | bytes 442376 | tf_op jit(solution)/shard_map/ppermute | solution.py:56
  8.2 18.8 %collective-permute-start.9 = (bf16[128,576]{1,0:T(8,128)(2,1)}, bf16[128,576]{1,0:T(8,128)(2,1)}, u32[]{:S(2)}, u32[]{:S(2)}) collective-permute-start(bf16[128,576]{1,0:T(8,128)(2,1)} %bitcast.59.clone.2), channel_id=1, source_target_pairs={{0,96},{4,100},{8,104},{12,108},{16,112},{20,116},{24,120},{28,124... | collective-permute-start | bytes 442376 | tf_op jit(solution)/shard_map/ppermute | solution.py:56
  9.6 19.7 %collective-permute-start.1 = (bf16[128,576]{1,0:T(8,128)(2,1)}, bf16[128,576]{1,0:T(8,128)(2,1)S(1)}, u32[]{:S(2)}, u32[]{:S(2)}) collective-permute-start(bf16[128,576]{1,0:T(8,128)(2,1)} %bitcast.61.clone.2), channel_id=1, source_target_pairs={{0,8},{4,12},{8,16},{12,20},{16,24},{20,28},{24,0},{28,4},{32,40},... | collective-permute-start | bytes 442376 | tf_op jit(solution)/shard_map/ppermute | solution.py:56
  12.3 18.8 %collective-permute-start.2 = (bf16[128,576]{1,0:T(8,128)(2,1)}, bf16[128,576]{1,0:T(8,128)(2,1)}, u32[]{:S(2)}, u32[]{:S(2)}) collective-permute-start(bf16[128,576]{1,0:T(8,128)(2,1)} %bitcast.61.clone.2), channel_id=1, source_target_pairs={{0,16},{4,20},{8,24},{12,28},{16,0},{20,4},{24,8},{28,12},{32,48},... | collective-permute-start | bytes 442376 | tf_op jit(solution)/shard_map/ppermute | solution.py:56
  16.3 15.9 %collective-permute-start.3 = (bf16[128,576]{1,0:T(8,128)(2,1)}, bf16[128,576]{1,0:T(8,128)(2,1)}, u32[]{:S(2)}, u32[]{:S(2)}) collective-permute-start(bf16[128,576]{1,0:T(8,128)(2,1)} %bitcast.61.clone.2), channel_id=1, source_target_pairs={{0,24},{4,28},{8,0},{12,4},{16,8},{20,12},{24,16},{28,20},{32,56},... | collective-permute-start | bytes 442376 | tf_op jit(solution)/shard_map/ppermute | solution.py:56
  29.4 16.2 %collective-permute-start.10 = (bf16[4,128,576]{1,2,0:T(8,128)(2,1)}, bf16[4,128,576]{1,2,0:T(8,128)(2,1)}, u32[]{:S(2)}, u32[]{:S(2)}) collective-permute-start(bf16[4,128,576]{1,2,0:T(8,128)(2,1)} %copy.165), channel_id=1, source_target_pairs={{0,8},{4,12},{8,16},{12,20},{16,24},{20,28},{24,0},{28,4},{32,40},... | collective-permute-start | bytes 1769480 | tf_op jit(solution)/shard_map/ppermute | solution.py:56
  29.4 27.0 %collective-permute-start.11 = (bf16[4,128,576]{1,2,0:T(8,128)(2,1)}, bf16[4,128,576]{1,2,0:T(8,128)(2,1)}, u32[]{:S(2)}, u32[]{:S(2)}) collective-permute-start(bf16[4,128,576]{1,2,0:T(8,128)(2,1)} %copy.165), channel_id=1, source_target_pairs={{0,16},{4,20},{8,24},{12,28},{16,0},{20,4},{24,8},{28,12},{32,48},... | collective-permute-start | bytes 1769480 | tf_op jit(solution)/shard_map/ppermute | solution.py:56
  31.1 30.7 %collective-permute-start.12 = (bf16[4,128,576]{1,2,0:T(8,128)(2,1)}, bf16[4,128,576]{1,2,0:T(8,128)(2,1)}, u32[]{:S(2)}, u32[]{:S(2)}) collective-permute-start(bf16[4,128,576]{1,2,0:T(8,128)(2,1)} %copy.165), channel_id=1, source_target_pairs={{0,24},{4,28},{8,0},{12,4},{16,8},{20,12},{24,16},{28,20},{32,56},... | collective-permute-start | bytes 1769480 | tf_op jit(solution)/shard_map/ppermute | solution.py:56
  34.5 29.5 %collective-permute-start.4 = (bf16[4,128,576]{1,2,0:T(8,128)(2,1)}, bf16[4,128,576]{1,2,0:T(8,128)(2,1)}, u32[]{:S(2)}, u32[]{:S(2)}) collective-permute-start(bf16[4,128,576]{1,2,0:T(8,128)(2,1)} %copy.157), channel_id=1, source_target_pairs={{0,32},{4,36},{8,40},{12,44},{16,48},{20,52},{24,56},{28,60},{32,6... | collective-permute-start | bytes 1769480 | tf_op jit(solution)/shard_map/ppermute | solution.py:56
  45.6 20.6 %collective-permute-start.5 = (bf16[4,128,576]{1,2,0:T(8,128)(2,1)}, bf16[4,128,576]{1,2,0:T(8,128)(2,1)}, u32[]{:S(2)}, u32[]{:S(2)}) collective-permute-start(bf16[4,128,576]{1,2,0:T(8,128)(2,1)} %copy.157), channel_id=1, source_target_pairs={{0,64},{4,68},{8,72},{12,76},{16,80},{20,84},{24,88},{28,92},{32,9... | collective-permute-start | bytes 1769480 | tf_op jit(solution)/shard_map/ppermute | solution.py:56
  56.4 16.8 %collective-permute-start.6 = (bf16[4,128,576]{1,2,0:T(8,128)(2,1)}, bf16[4,128,576]{1,2,0:T(8,128)(2,1)}, u32[]{:S(2)}, u32[]{:S(2)}) collective-permute-start(bf16[4,128,576]{1,2,0:T(8,128)(2,1)} %copy.157), channel_id=1, source_target_pairs={{0,96},{4,100},{8,104},{12,108},{16,112},{20,116},{24,120},{28,124... | collective-permute-start | bytes 1769480 | tf_op jit(solution)/shard_map/ppermute | solution.py:56
  114.1 24.6 %all-to-all-start = ((bf16[16,272,128]{2,1,0:T(8,128)(2,1)}), bf16[16,272,128]{2,1,0:T(8,128)(2,1)}, u32[]{:S(2)}, u32[]{:S(2)}) async-start(bf16[16,272,128]{2,1,0:T(8,128)(2,1)} %far.1), calls=%async_computation | async-start | bytes 2228224 | tf_op jit(solution)/shard_map/all_to_all | solution.py:65
  118.8 48.8 %collective-permute-start.14 = (bf16[4096,224]{0,1:T(8,128)(2,1)}, bf16[4096,224]{0,1:T(8,128)(2,1)}, u32[]{:S(2)}, u32[]{:S(2)}) collective-permute-start(bf16[4096,224]{0,1:T(8,128)(2,1)} %param.21), channel_id=1, source_target_pairs={{0,4},{4,0},{8,12},{12,8},{16,20},{20,16},{24,28},{28,24},{32,36},... | collective-permute-start | bytes 5505032 | tf_op jit(solution)/shard_map/ppermute | solution.py:52
  133.0 54.6 %collective-permute-start.20 = (bf16[2,3,224,1024]{3,2,1,0:T(8,128)(2,1)}, bf16[2,3,224,1024]{3,2,1,0:T(8,128)(2,1)}, u32[]{:S(2)}, u32[]{:S(2)}) collective-permute-start(bf16[2,3,224,1024]{3,2,1,0:T(8,128)(2,1)} %bitcast.84), channel_id=1, source_target_pairs={{0,4},{4,0},{8,12},{12,8},{16,20},{20,16},{24,28},{28,24},{32,36},... | collective-permute-start | bytes 8257544 | tf_op jit(solution)/shard_map/ppermute | solution.py:52
  142.1 22.9 %all-to-all-start.1 = ((bf16[16,8,4096]{2,1,0:T(8,128)(2,1)}), bf16[16,8,4096]{2,1,0:T(8,128)(2,1)}, u32[]{:S(2)}, u32[]{:S(2)}) async-start(bf16[16,8,4096]{2,1,0:T(8,128)(2,1)} %combine.1), calls=%async_computation.1 | async-start | bytes 2097152 | tf_op jit(solution)/shard_map/all_to_all | solution.py:65
  148.8 27.1 %collective-permute-start = (bf16[256,224]{1,0:T(8,128)(2,1)S(1)}, bf16[256,224]{1,0:T(8,128)(2,1)S(1)}, u32[]{:S(2)}, u32[]{:S(2)}) collective-permute-start(bf16[256,224]{1,0:T(8,128)(2,1)S(1)} %copy.153), channel_id=1, source_target_pairs={{0,4},{4,0},{8,12},{12,8},{16,20},{20,16},{24,28},{28,24},{32,36},... | collective-permute-start | bytes 344072 | tf_op jit(solution)/shard_map/ppermute | solution.py:52
  170.2 9.0 %collective-permute-start.15 = (bf16[2,128,224]{2,1,0:T(8,128)(2,1)S(1)}, bf16[2,128,224]{2,1,0:T(8,128)(2,1)S(1)}, u32[]{:S(2)}, u32[]{:S(2)}) collective-permute-start(bf16[2,128,224]{2,1,0:T(8,128)(2,1)S(1)} %pad_maximum_fusion.4), channel_id=1, source_target_pairs={{0,2},{1,3},{2,0},{3,1},{4,6},{5,7},{6,4},{7,5},{8,10},{9,11},{10,... | collective-permute-start | bytes 344072 | tf_op jit(solution)/shard_map/ppermute | solution.py:60
  173.2 6.5 %collective-permute-start.16 = (bf16[2,128,224]{2,1,0:T(8,128)(2,1)S(1)}, bf16[2,128,224]{2,1,0:T(8,128)(2,1)S(1)}, u32[]{:S(2)}, u32[]{:S(2)}) collective-permute-start(bf16[2,128,224]{2,1,0:T(8,128)(2,1)S(1)} %pad_maximum_fusion.4), channel_id=1, source_target_pairs={{0,1},{1,2},{2,3},{3,0},{4,5},{5,6},{6,7},{7,4},{8,9},{9,10},{10,1... | collective-permute-start | bytes 344072 | tf_op jit(solution)/shard_map/ppermute | solution.py:60
  173.6 6.1 %collective-permute-start.17 = (bf16[2,128,224]{2,1,0:T(8,128)(2,1)S(1)}, bf16[2,128,224]{2,1,0:T(8,128)(2,1)S(1)}, u32[]{:S(2)}, u32[]{:S(2)}) collective-permute-start(bf16[2,128,224]{2,1,0:T(8,128)(2,1)S(1)} %pad_maximum_fusion.4), channel_id=1, source_target_pairs={{0,3},{1,0},{2,1},{3,2},{4,7},{5,4},{6,5},{7,6},{8,11},{9,8},{10,9... | collective-permute-start | bytes 344072 | tf_op jit(solution)/shard_map/ppermute | solution.py:60
  176.0 11.6 %collective-permute-start.21 = (bf16[2,224,256]{2,1,0:T(8,128)(2,1)S(1)}, bf16[2,224,256]{2,1,0:T(8,128)(2,1)S(1)}, u32[]{:S(2)}, u32[]{:S(2)}) collective-permute-start(bf16[2,224,256]{2,1,0:T(8,128)(2,1)S(1)} %bitcast.104), channel_id=1, source_target_pairs={{0,4},{4,0},{8,12},{12,8},{16,20},{20,16},{24,28},{28,24},{32,36},... | collective-permute-start | bytes 688136 | tf_op jit(solution)/shard_map/ppermute | solution.py:52
  179.2 7.8 %collective-permute-start.19 = (bf16[224]{0:T(256)(128)(2,1)S(1)}, bf16[224]{0:T(256)(128)(2,1)S(1)}, u32[]{:S(2)}, u32[]{:S(2)}) collective-permute-start(bf16[224]{0:T(256)(128)(2,1)S(1)} %copy-done.26), channel_id=1, source_target_pairs={{0,4},{4,0},{8,12},{12,8},{16,20},{20,16},{24,28},{28,24},{32,36},... | collective-permute-start | bytes 1352 | tf_op jit(solution)/shard_map/ppermute | solution.py:52
  179.8 7.8 %collective-permute-start.18 = (f32[2,128,224]{2,1,0:T(8,128)S(1)}, f32[2,128,224]{2,1,0:T(8,128)S(1)}, u32[]{:S(2)}, u32[]{:S(2)}) collective-permute-start(f32[2,128,224]{2,1,0:T(8,128)S(1)} %add_add_fusion.own_ref), channel_id=1, source_target_pairs={{0,4},{4,0},{8,12},{12,8},{16,20},{20,16},{24,28},{28,24},{32,36},... | collective-permute-start | bytes 688136 | tf_op jit(solution)/shard_map/ppermute | solution.py:52
  195.0 46.2 %all-to-all-start.2 = ((bf16[16,656,128]{2,1,0:T(8,128)(2,1)}), bf16[16,656,128]{2,1,0:T(8,128)(2,1)S(1)}, u32[]{:S(2)}, u32[]{:S(2)}) async-start(bf16[16,656,128]{2,1,0:T(8,128)(2,1)} %gate_up.1), calls=%async_computation.2 | async-start | bytes 5373952 | tf_op jit(solution)/shard_map/all_to_all | solution.py:65
  202.6 55.0 %collective-permute-start.22 = (bf16[3,1024,224]{1,2,0:T(8,128)(2,1)}, bf16[3,1024,224]{1,2,0:T(8,128)(2,1)}, u32[]{:S(2)}, u32[]{:S(2)}) collective-permute-start(bf16[3,1024,224]{1,2,0:T(8,128)(2,1)} %get-tuple-element.17), channel_id=1, source_target_pairs={{0,4},{4,0},{8,12},{12,8},{16,20},{20,16},{24,28},{28,24},{32,36},... | collective-permute-start | bytes 4128776 | tf_op jit(solution)/shard_map/ppermute | solution.py:52
  246.8 22.7 %all-to-all-start.3 = ((bf16[16,320,128]{2,1,0:T(8,128)(2,1)}), bf16[16,320,128]{2,1,0:T(8,128)(2,1)S(1)}, u32[]{:S(2)}, u32[]{:S(2)}) async-start(bf16[16,320,128]{2,1,0:T(8,128)(2,1)} %activate.1), calls=%async_computation.3 | async-start | bytes 2621440 | tf_op jit(solution)/shard_map/all_to_all | solution.py:65
  251.0 9.1 %collective-permute-start.23 = (bf16[256,224]{1,0:T(8,128)(2,1)S(1)}, bf16[256,224]{1,0:T(8,128)(2,1)S(1)}, u32[]{:S(2)}, u32[]{:S(2)}) collective-permute-start(bf16[256,224]{1,0:T(8,128)(2,1)S(1)} %copy.201), channel_id=1, source_target_pairs={{0,4},{4,0},{8,12},{12,8},{16,20},{20,16},{24,28},{28,24},{32,36},... | collective-permute-start | bytes 344072 | tf_op jit(solution)/shard_map/ppermute | solution.py:52
  275.0 4.3 %collective-permute-start.24 = (bf16[256,224]{1,0:T(8,128)(2,1)}, bf16[256,224]{1,0:T(8,128)(2,1)S(1)}, u32[]{:S(2)}, u32[]{:S(2)}) collective-permute-start(bf16[256,224]{1,0:T(8,128)(2,1)} %get-tuple-element.12), channel_id=1, source_target_pairs={{0,4},{4,0},{8,12},{12,8},{16,20},{20,16},{24,28},{28,24},{32,36},... | collective-permute-start | bytes 344072 | tf_op jit(solution)/shard_map/ppermute | solution.py:52
  280.2 6.3 %collective-permute-start.25 = (bf16[256,224]{1,0:T(8,128)(2,1)S(1)}, bf16[256,224]{1,0:T(8,128)(2,1)S(1)}, u32[]{:S(2)}, u32[]{:S(2)}) collective-permute-start(bf16[256,224]{1,0:T(8,128)(2,1)S(1)} %add_convert_fusion), channel_id=1, source_target_pairs={{0,2},{1,3},{2,0},{3,1},{4,6},{5,7},{6,4},{7,5},{8,10},{9,11},{10,... | collective-permute-start | bytes 344072 | tf_op jit(solution)/shard_map/ppermute | solution.py:60
  281.0 9.1 %collective-permute-start.26 = (bf16[256,224]{1,0:T(8,128)(2,1)S(1)}, bf16[256,224]{1,0:T(8,128)(2,1)S(1)}, u32[]{:S(2)}, u32[]{:S(2)}) collective-permute-start(bf16[256,224]{1,0:T(8,128)(2,1)S(1)} %add_convert_fusion), channel_id=1, source_target_pairs={{0,1},{1,2},{2,3},{3,0},{4,5},{5,6},{6,7},{7,4},{8,9},{9,10},{10,1... | collective-permute-start | bytes 344072 | tf_op jit(solution)/shard_map/ppermute | solution.py:60
  283.9 6.1 %collective-permute-start.27 = (bf16[256,224]{1,0:T(8,128)(2,1)S(1)}, bf16[256,224]{1,0:T(8,128)(2,1)S(1)}, u32[]{:S(2)}, u32[]{:S(2)}) collective-permute-start(bf16[256,224]{1,0:T(8,128)(2,1)S(1)} %add_convert_fusion), channel_id=1, source_target_pairs={{0,3},{1,0},{2,1},{3,2},{4,7},{5,4},{6,5},{7,6},{8,11},{9,8},{10,9... | collective-permute-start | bytes 344072 | tf_op jit(solution)/shard_map/ppermute | solution.py:60
  (27 other events, 241.0 us)

commit v2 on v1

v2 whole, which is shorter than its diff:
```python
import functools
import math

import jax
import jax.numpy as jnp
from jax import lax
from jax.experimental import pallas as pl
from jax.experimental.pallas import tpu as pltpu
from jax.sharding import PartitionSpec as P

D = 7168
LAT = 512
ROPE = 64
HD = 128
DRAFT = 8
EXP_DEV = 3
CAP = 192
RING = 4
CHIPS = 16
HEADS = 32
ROWS = HEADS * DRAFT
MSG = ROWS + 16
HALF = ROWS // 2
WIDTH = LAT + ROPE
QROWS = HALF * WIDTH // 128
GATE = 336
UP = 320
ACT = 320
KEXP = (HD + ROPE) ** (-0.5) * math.log2(math.e)
BF = jnp.bfloat16
F32 = jnp.float32


def device_of(z, x, c):
    return (z * RING + x) * 2 + c


def pre_pairs(move):
    return [
        (device_of(z, x, c), device_of(*move(z, x, c)))
        for z in range(RING)
        for x in range(RING)
        for c in range(2)
    ]


CORE = pre_pairs(lambda z, x, c: (z, x, 1 - c))
X_BY = {d: pre_pairs(lambda z, x, c: (z, (x + d) % RING, c)) for d in (1, 2, 3)}
Z_BY = {d: pre_pairs(lambda z, x, c: ((z + d) % RING, x, c)) for d in (1, 2, 3)}
Y_BY = {d: [(e, (e + d) % RING) for e in range(RING)] for d in (1, 2, 3)}
NEAR_SPOTS = [(0, 0)] + [(dz, dx) for dz in (0, 1, 3) for dx in (0, 1, 3) if dz or dx]
FAR_SPOTS = [(dz, dx) for dz in range(RING) for dx in range(RING) if 2 in (dz, dx)]
SAME_CORE = [[chip * 2 + c for chip in range(CHIPS)] for c in range(2)]


def swap_core(value):
    return lax.ppermute(value, "pre", CORE)


def ring_send(values, pairs):
    return [lax.ppermute(value, "pre", pairs[d]) for d, value in zip((1, 2, 3), values)]


def exp_sum(value):
    others = {d: lax.ppermute(value, "exp", Y_BY[d]).astype(F32) for d in (2, 1, 3)}
    return (value.astype(F32) + others[2]) + (others[1] + others[3])


def chip_exchange(value):
    return lax.all_to_all(value, "pre", 0, 0, axis_index_groups=SAME_CORE)


def dot(a, b, dims=((1,), (0,))):
    return lax.dot_general(a, b, (dims, ((), ())), preferred_element_type=F32)


NT = ((1,), (1,))


def eye(n):
    return lax.broadcasted_iota(jnp.int32, (n, n), 0) == lax.broadcasted_iota(jnp.int32, (n, n), 1)


def column_to_rows(column):
    mask = eye(128)
    parts = [
        jnp.sum(jnp.where(mask, jnp.broadcast_to(column[b * 128 : (b + 1) * 128], (128, 128)), 0.0), 0, keepdims=True)
        for b in range(column.shape[0] // 128)
    ]
    return jnp.concatenate(parts, 0)


def three_terms(rows):
    high = rows.astype(BF).astype(F32)
    rest = rows - high
    mid = rest.astype(BF).astype(F32)
    return [high, mid, rest - mid]


def near_kernel(q_ref, k_ref, w_ref, out_ref, stat_ref, acc):
    keys = k_ref[...]
    scores = dot(q_ref[...], keys, NT)
    draft = lax.broadcasted_iota(jnp.int32, scores.shape, 0) % DRAFT
    key = lax.broadcasted_iota(jnp.int32, scores.shape, 1)
    allowed = key <= draft
    top = jnp.max(jnp.where(allowed, scores, -jnp.inf), 1, keepdims=True)
    weight = jnp.where(allowed, jnp.exp2((scores - top) * KEXP), 0.0).astype(BF)
    total = jnp.sum(weight.astype(F32), 1, keepdims=True)
    acc[...] = dot(weight, keys[:, :LAT])
    stat_ref[...] = jnp.concatenate([column_to_rows(top), column_to_rows(total)], 0)
    for h in range(HEADS):
        rows = slice(h * DRAFT, (h + 1) * DRAFT)
        out_ref[rows, :] = dot(acc[rows, :].astype(BF), w_ref[h])


SLOTS = CHIPS // 2


def attend(q_ref, la_ref, lb_ref, out_ref, stat_ref):
    parts = []
    for b in range(4):
        rows = slice(b * HALF, (b + 1) * HALF)
        parts.append(jnp.concatenate([q_ref[0, rows, :], q_ref[1, rows, :]], 0))
    ropes = [q_ref[half, 4 * HALF : QROWS, :] for half in range(2)]
    parts.append(jnp.concatenate([r[:, s : s + ROPE] for r in ropes for s in (0, ROPE)], 0))
    q = jnp.concatenate(parts, 1)
    sa = dot(q, la_ref[...])
    sb = dot(q, lb_ref[...])
    top = jnp.max(jnp.maximum(sa, sb), 1, keepdims=True)
    wa = jnp.exp2((sa - top) * KEXP).astype(BF)
    wb = jnp.exp2((sb - top) * KEXP).astype(BF)
    total = jnp.sum(wa.astype(F32) + wb.astype(F32), 1, keepdims=True)
    out_ref[...] = (dot(wa, la_ref[:LAT], NT) + dot(wb, lb_ref[:LAT], NT)).astype(BF)
    stat_ref[...] = jnp.concatenate(
        [column_to_rows(top), column_to_rows(total), jnp.zeros((4, 128), F32)], 0
    )


def attend_all(plan, prompt, sources, la_ref, lb_ref, q_ref, sems, out_ref, stat_ref):
    for n, spots in enumerate(plan):
        for half, (source, at) in enumerate(spots):
            pltpu.make_async_copy(sources[source].at[at], q_ref.at[n, half], sems.at[n, half]).start()

    @pl.loop(0, SLOTS // 2)
    def _(pair):
        for r in range(2):
            n = pair * 2 + r
            for half in range(2):
                pltpu.make_async_copy(sources[0].at[0], q_ref.at[n, half], sems.at[n, half]).wait()
            which = prompt[n]
            attend(q_ref.at[n], la_ref.at[which], lb_ref.at[which], out_ref.at[n], stat_ref.at[n])


def far_first_kernel(plan, prompt, *refs):
    sources = refs[: -6]
    la_ref, lb_ref, out_ref, stat_ref, q_ref, sems = refs[-6:]
    attend_all(plan, prompt, sources, la_ref, lb_ref, q_ref, sems, out_ref, stat_ref)


def far_second_kernel(plan, prompt, place, *refs):
    sources = refs[: -11]
    la_ref, lb_ref, w_ref, early_ref, early_stat, msg_ref, q_ref, acc, stat, sems, early_sem = refs[-11:]
    fetch = pltpu.make_async_copy(early_ref, acc.at[pl.ds(0, SLOTS)], early_sem)
    fetch.start()
    attend_all(
        plan,
        prompt,
        sources,
        la_ref,
        lb_ref,
        q_ref,
        sems,
        acc.at[pl.ds(SLOTS, SLOTS)],
        stat,
    )
    fetch.wait()
    for n in range(CHIPS):
        rows = early_stat[n] if n < SLOTS else stat[n - SLOTS]
        extra = three_terms(rows[0:2]) + three_terms(rows[2:4]) + [jnp.zeros((4, 128), F32)]
        msg_ref[place[n], ROWS:MSG, :] = jnp.concatenate(extra, 0).astype(BF)
    low = lax.broadcasted_iota(jnp.int32, (CHIPS * 16, HD), 0) % 16 < DRAFT

    @pl.loop(0, HEADS // 4)
    def _(quad):
        for r in range(2):
            pair = quad * 2 + r
            start = pl.multiple_of(pair * 16, 16)
            rows = acc[:, pl.ds(start, 16), :].reshape(CHIPS * 16, LAT)
            both = dot(rows, jnp.concatenate([w_ref[pair * 2], w_ref[pair * 2 + 1]], 1))
            picked = jnp.where(low, both[:, :HD], both[:, HD:]).astype(BF)
            for n in range(CHIPS):
                msg_ref[place[n], pl.ds(start, 16), :] = picked[n * 16 : (n + 1) * 16]


def combine_kernel(rec_ref, near_ref, stat_ref, out_ref):
    tops, totals = [], []
    for p in range(CHIPS):
        extra = rec_ref[p, ROWS:MSG, :].astype(F32)
        tops.append(extra[0:2] + extra[2:4] + extra[4:6])
        totals.append(extra[6:8] + extra[8:10] + extra[10:12])
    tops.append(stat_ref[0:2])
    totals.append(stat_ref[2:4])
    best = functools.reduce(jnp.maximum, tops)
    scale = [jnp.exp2((t - best) * KEXP) for t in tops]
    whole = functools.reduce(jnp.add, [s * t for s, t in zip(scale, totals)])
    scale = [s / whole for s in scale]
    blocks = []
    for b in range(2):
        table = jnp.concatenate(
            [s[b : b + 1] for s in scale] + [jnp.zeros((128 - len(scale), 128), F32)], 0
        ).T
        rows = slice(b * 128, (b + 1) * 128)
        value = near_ref[rows, :] * table[:, CHIPS : CHIPS + 1]
        for p in range(CHIPS):
            value = value + rec_ref[p, rows, :].astype(F32) * table[:, p : p + 1]
        blocks.append(value)
    value = jnp.concatenate(blocks, 0)
    flat = jnp.concatenate([value[h * DRAFT : (h + 1) * DRAFT] for h in range(HEADS)], 1).astype(BF)
    for p in range(CHIPS):
        out_ref[p] = flat


def project_kernel(head_ref, wm_ref, wo_ref, out_ref, acc):
    k = pl.program_id(0)
    head = head_ref[...]
    part = jnp.concatenate([dot(wm_ref[...], head, NT), dot(wo_ref[...], head, NT)], 0)

    @pl.when(k == 0)
    def _():
        acc[...] = part

    @pl.when(k > 0)
    def _():
        acc[...] += part

    @pl.when(k == pl.num_programs(0) - 1)
    def _():
        out_ref[...] = acc[...].astype(BF)


def gate_up_kernel(
    at_ref, own_ref, rcv_ref, gm_ref, go_ref, pick_ref, wm_ref, wo_ref, sm_ref, so_ref, *refs
):
    outs, (xm, xo, pair, wide) = refs[:8], refs[8:]
    e = pl.program_id(0)
    core, z, x = at_ref[0], at_ref[1], at_ref[2]
    n = xm.shape[0]

    def destinations():
        for dx in range(RING):
            for dz in range(RING):
                chip = lax.rem(z + dz, RING) * RING + lax.rem(x + dx, RING)
                yield (outs[dx].at[dz], outs[RING + dz].at[dx]), chip

    @pl.when(e == 0)
    def _():
        square = jnp.zeros((1, 256), F32)
        for keep, gain_ref, mine, theirs in ((xm, gm_ref, 0, n), (xo, go_ref, n, 0)):
            own = own_ref[mine : mine + n, :]
            rcv = rcv_ref[theirs : theirs + n, :]
            whole = jnp.concatenate([jnp.where(core == 0, own, rcv), jnp.where(core == 0, rcv, own)], 1)
            square = square + jnp.sum(whole * whole, 0, keepdims=True)
            keep[...] = (whole * gain_ref[...]).astype(BF)
        terms = three_terms(jnp.concatenate([square[:, :128], square[:, 128:]], 0))
        rows = jnp.concatenate(terms + [jnp.zeros((10, 128), F32)], 0).astype(BF)
        same = eye(256).astype(BF)
        all_m = dot(same, xm[...], NT).astype(BF)
        all_o = dot(same, xo[...], NT).astype(BF)
        for g in range(2):
            pair[g] = (dot(all_m, sm_ref[g]) + dot(all_o, so_ref[g])).astype(BF)
        for pieces, chip in destinations():
            pieces[0][320:336, :] = rows
            top = pl.multiple_of(lax.rem(chip, 8) * 32, 32)
            left = pl.multiple_of(lax.div(chip, 8) * 128, 128)
            for g in range(2):
                pieces[g][288:320, :] = pair[g, pl.ds(top, 32), pl.ds(left, 128)]

    picked_m = dot(pick_ref[0], xm[...], NT).astype(BF)
    picked_o = dot(pick_ref[0], xo[...], NT).astype(BF)
    for g in range(2):
        wide[g] = (dot(picked_m, wm_ref[g, 0]) + dot(picked_o, wo_ref[g, 0])).astype(BF)
    start = pl.multiple_of(e * 96, 32)
    for pieces, chip in destinations():
        top = pl.multiple_of(lax.rem(chip, 2) * 96, 32)
        left = pl.multiple_of(lax.div(chip, 2) * 128, 128)
        for g in range(2):
            pieces[g][pl.ds(start, 96), :] = wide[g, pl.ds(top, 96), pl.ds(left, 128)]


def fold_kernel(*refs):
    for k in range(RING):
        total = refs[0][k].astype(F32)
        for r in refs[1:RING]:
            total = total + r[k].astype(F32)
        refs[RING + k][...] = total.astype(BF)


def act_kernel(*refs):
    gates, ups, pick_ref, out_ref = refs[:RING], refs[RING : 2 * RING], refs[-2], refs[-1]

    def total(parts):
        return functools.reduce(jnp.add, [part[...].astype(F32) for part in parts])

    gate, up = total(gates), total(ups)
    square = gate[320:322] + gate[322:324] + gate[324:326]
    inverse = lax.rsqrt(square / D + 1e-06)
    pick = pick_ref[...].astype(F32)
    factor = jnp.sum(pick[:, :128] * inverse[0:1] + pick[:, 128:] * inverse[1:2], 1, keepdims=True)
    act = (jax.nn.silu(gate[:ACT] * factor) * (up * factor)).astype(BF)
    for p in range(CHIPS):
        out_ref[p] = act


def down_kernel(act_ref, wm_ref, wo_ref, sm_ref, so_ref, weight_ref, pick_ref, mine_ref, other_ref):
    pieces = []
    for e in range(EXP_DEV):
        rows = slice(e * 96, (e + 1) * 96)
        pieces.append(
            jnp.concatenate(
                [jnp.concatenate([act_ref[u * 2 + half, rows, :] for u in range(8)], 1) for half in range(2)], 0
            )
        )
    shared = jnp.concatenate(
        [jnp.concatenate([act_ref[u * 8 + t, 288:320, :] for u in range(2)], 1) for t in range(8)], 0
    )
    for w_ref, s_ref, out_ref in ((wm_ref, sm_ref, mine_ref), (wo_ref, so_ref, other_ref)):
        total = dot(s_ref[...], shared, NT)
        for e in range(EXP_DEV):
            weighted = (dot(w_ref[e], pieces[e], NT) * weight_ref[e]).astype(BF)
            total = total + dot(weighted, pick_ref[e])
        out_ref[...] = total.astype(out_ref.dtype)


def params(n=0, limit=24):
    size = limit * 1024 * 1024
    if n:
        return pltpu.CompilerParams(vmem_limit_bytes=size, dimension_semantics=("arbitrary",) * n)
    return pltpu.CompilerParams(vmem_limit_bytes=size)


def shape(*dims, dtype=BF):
    return jax.ShapeDtypeStruct(dims, dtype)


def whole(*dims):
    return pl.BlockSpec(dims, lambda *at: (0,) * len(dims))


def near_part(q, keys, w_uv):
    return pl.pallas_call(
        near_kernel,
        out_shape=(shape(ROWS, HD, dtype=F32), shape(4, 128, dtype=F32)),
        scratch_shapes=[pltpu.VMEM((ROWS, LAT), F32)],
        compiler_params=params(),
        name="near",
    )(q, keys, w_uv)


def vmem():
    return pl.BlockSpec(memory_space=pltpu.VMEM)


def far_cost():
    rows = SLOTS * ROWS
    return pl.CostEstimate(
        flops=2 * rows * 1024 * (WIDTH + LAT), bytes_accessed=24 * 1024 * 1024, transcendentals=rows * 1024
    )


def far_first(plan, prompt, sources, la, lb):
    return pl.pallas_call(
        functools.partial(far_first_kernel, plan),
        out_shape=(shape(SLOTS, ROWS, LAT), shape(SLOTS, 8, 128, dtype=F32)),
        in_specs=[pl.BlockSpec(memory_space=pltpu.SMEM)]
        + [pl.BlockSpec(memory_space=pl.ANY)] * len(sources)
        + [vmem(), vmem()],
        out_specs=(vmem(), vmem()),
        scratch_shapes=[
            pltpu.VMEM((SLOTS, 2, QROWS, 128), BF),
            pltpu.SemaphoreType.DMA((SLOTS, 2)),
        ],
        compiler_params=params(limit=26),
        cost_estimate=far_cost(),
        name="far_first",
    )(prompt, *sources, la, lb)


def far_second(plan, prompt, place, sources, la, lb, w_uv, early, early_stat):
    return pl.pallas_call(
        functools.partial(far_second_kernel, plan),
        out_shape=shape(CHIPS, MSG, HD),
        in_specs=[pl.BlockSpec(memory_space=pltpu.SMEM)] * 2
        + [pl.BlockSpec(memory_space=pl.ANY)] * len(sources)
        + [vmem(), vmem(), vmem(), pl.BlockSpec(memory_space=pl.ANY), vmem()],
        out_specs=vmem(),
        scratch_shapes=[
            pltpu.VMEM((SLOTS, 2, QROWS, 128), BF),
            pltpu.VMEM((CHIPS, ROWS, LAT), BF),
            pltpu.VMEM((SLOTS, 8, 128), F32),
            pltpu.SemaphoreType.DMA((SLOTS, 2)),
            pltpu.SemaphoreType.DMA,
        ],
        compiler_params=params(limit=36),
        cost_estimate=far_cost(),
        name="far_second",
    )(prompt, place, *sources, la, lb, w_uv, early, early_stat)


def combine(received, near_out, near_stat):
    return pl.pallas_call(
        combine_kernel,
        out_shape=shape(CHIPS, DRAFT, HEADS * HD),
        compiler_params=params(),
        name="combine",
    )(received, near_out, near_stat)


def project(head, wm, wo):
    n, depth = wm.shape
    step = depth // 4
    return pl.pallas_call(
        project_kernel,
        out_shape=shape(2 * n, head.shape[0]),
        grid=(4,),
        in_specs=[
            pl.BlockSpec((head.shape[0], step), lambda k: (0, k)),
            pl.BlockSpec((n, step), lambda k: (0, k)),
            pl.BlockSpec((n, step), lambda k: (0, k)),
        ],
        out_specs=whole(2 * n, head.shape[0]),
        scratch_shapes=[pltpu.VMEM((2 * n, head.shape[0]), F32)],
        compiler_params=params(1),
        name="project",
    )(head, wm, wo)


def gate_up(at, own, rcv, gain_m, gain_o, pick, wm, wo, sm, so):
    n, half = wm.shape[2:]
    weights = pl.BlockSpec((2, 1, n, half), lambda e, c: (0, e, 0, 0))
    return pl.pallas_call(
        gate_up_kernel,
        out_shape=[shape(RING, GATE, 128)] * RING + [shape(RING, UP, 128)] * RING,
        grid_spec=pltpu.PrefetchScalarGridSpec(
            num_scalar_prefetch=1,
            grid=(EXP_DEV,),
            in_specs=[
                whole(*own.shape),
                whole(*rcv.shape),
                whole(n, 1),
                whole(n, 1),
                pl.BlockSpec((1, CAP, 256), lambda e, c: (e, 0, 0)),
                weights,
                weights,
                whole(*sm.shape),
                whole(*so.shape),
            ],
            out_specs=[whole(RING, GATE, 128)] * RING + [whole(RING, UP, 128)] * RING,
            scratch_shapes=[
                pltpu.VMEM((n, 256), BF),
                pltpu.VMEM((n, 256), BF),
                pltpu.VMEM((2, 256, 256), BF),
                pltpu.VMEM((2, CAP, half), BF),
            ],
        ),
        compiler_params=params(1),
        name="gate_up",
    )(at, own, rcv, gain_m, gain_o, pick, wm, wo, sm, so)


def fold(parts):
    return pl.pallas_call(
        fold_kernel,
        out_shape=[shape(*parts[0].shape[1:])] * RING,
        compiler_params=params(),
        name="fold",
    )(*parts)


def activate(gates, ups, pick):
    return pl.pallas_call(
        act_kernel,
        out_shape=shape(CHIPS, ACT, 128),
        compiler_params=params(),
        name="activate",
    )(*gates, *ups, pick)


def down(acts, wm, wo, sm, so, weight, pick):
    n = wm.shape[1]
    return pl.pallas_call(
        down_kernel,
        out_shape=(shape(n, 256, dtype=F32), shape(n, 256)),
        compiler_params=params(),
        name="down",
    )(acts, wm, wo, sm, so, weight, pick)


def halves(value, core, axis):
    size = value.shape[axis] // 2
    mine = lax.dynamic_slice_in_dim(value, core * size, size, axis)
    other = lax.dynamic_slice_in_dim(value, (1 - core) * size, size, axis)
    return mine, other


def by_core(value):
    tail = value.shape[1:]
    return value.reshape(CHIPS, 2, DRAFT, *tail).swapaxes(0, 1).reshape(2 * CHIPS * DRAFT, *tail)


def query_message(q):
    latent = q[:, :LAT].reshape(HALF, 4, 128).swapaxes(0, 1).reshape(4 * HALF, 128)
    rope = q[:, LAT:].reshape(2, HALF // 2, ROPE).swapaxes(0, 1).reshape(HALF // 2, 2 * ROPE)
    return jnp.concatenate([latent, rope], 0)


def per_device(
    queries,
    draft_latents,
    prefix_latents,
    prefix_of,
    accepted,
    w_uv,
    w_out,
    residual,
    norm_gain,
    w_gate_up,
    w_down,
    shared_gate_up,
    shared_down,
    expert_ids,
    expert_gates,
):
    pre = lax.axis_index("pre")
    core, chip = pre % 2, pre // 2
    z, x = chip // RING, chip % RING
    tokens = expert_ids.shape[0]

    q_own = queries[0].swapaxes(0, 1).reshape(ROWS, WIDTH)
    q_first = query_message(q_own[:HALF])
    q_second = query_message(q_own[HALF:])
    latents = prefix_latents.swapaxes(1, 2)
    latents_other = swap_core(latents)
    first = jnp.stack([q_first] + ring_send([q_first] * 3, X_BY))
    second = jnp.stack([q_second] + ring_send([q_second] * 3, Z_BY))
    first_1, first_3 = [lax.ppermute(first, "pre", Z_BY[d]) for d in (1, 3)]
    second_1, second_3 = [lax.ppermute(second, "pre", X_BY[d]) for d in (1, 3)]
    (first, w_out, residual, norm_gain, w_gate_up, w_down, shared_gate_up, shared_down, draft_latents) = (
        lax.optimization_barrier(
            (first, w_out, residual, norm_gain, w_gate_up, w_down, shared_gate_up, shared_down, draft_latents)
        )
    )
    pair_m, pair_send = halves(w_gate_up.transpose(2, 0, 1, 3), core, 3)
    shared_m, shared_send = halves(shared_gate_up.swapaxes(0, 1), core, 2)
    down_m, down_send = halves(w_down.swapaxes(1, 2), core, 2)
    shared_down_m, shared_down_send = halves(shared_down.T, core, 1)
    token = jnp.arange(tokens, dtype=jnp.int32)
    order = by_core(token)
    to_order = (token[:, None] == order[None, :]).astype(BF)
    skip_m, skip_send = halves(dot(residual.T, to_order).astype(BF), core, 1)
    gain_m = norm_gain[:, None]
    w_out = w_out.T
    live = by_core((jnp.arange(DRAFT)[None, :] < accepted[:, None]).reshape(tokens).astype(F32))
    local_experts = lax.axis_index("exp") * EXP_DEV + jnp.arange(EXP_DEV, dtype=jnp.int32)
    chosen = by_core(expert_ids)[:, :, None] == local_experts[None, None, :]
    routed = jnp.any(chosen, 1)
    weights = jnp.sum(jnp.where(chosen, by_core(expert_gates)[:, :, None], 0.0), 1) * live[:, None]
    position = jnp.cumsum(routed.astype(jnp.int32), 0) - 1
    slot_hit = routed.T[:, None, :] & (
        position.T[:, None, :] == jnp.arange(CAP, dtype=jnp.int32)[None, :, None]
    )
    pick = slot_hit.astype(BF)
    slot_weight = jnp.sum(jnp.where(slot_hit, weights.T[:, None, :], 0.0), 2)[:, None, :]
    my_slots = lax.dynamic_slice_in_dim(pick, (chip % 2) * 96, 96, 1).reshape(288, tokens)
    my_tokens = (token[None, :] == (chip % 8) * 32 + jnp.arange(32, dtype=jnp.int32)[:, None]).astype(BF)
    my_pick = jnp.concatenate([my_slots, my_tokens], 0)

    near_keys = jnp.pad(draft_latents[0], ((0, 128 - DRAFT), (0, 0)))
    near_out, near_stat = near_part(q_own, near_keys, w_uv)

    prepared = (pair_m, shared_m, down_m, shared_down_m, slot_weight, skip_m, gain_m, pick, my_pick, near_out, near_stat)
    sends = (pair_send, shared_send, down_send, shared_down_send, skip_send, gain_m, w_out)
    (first_1, first_3, second_1, second_3, prepared, sends) = lax.optimization_barrier(
        (first_1, first_3, second_1, second_3, prepared, sends)
    )
    pair_m, shared_m, down_m, shared_down_m, slot_weight, skip_m, gain_m, pick, my_pick, near_out, near_stat = prepared
    first_2 = [lax.ppermute(first_1[:2], "pre", Z_BY[1]), lax.ppermute(first_3[2:], "pre", Z_BY[3])]
    second_2 = [lax.ppermute(second_1[:2], "pre", X_BY[1]), lax.ppermute(second_3[2:], "pre", X_BY[3])]
    pair_o, shared_o, down_o, shared_down_o, skip_o, gain_o, w_out_o = [swap_core(v) for v in sends]
    w_out = sends[-1]
    skip = jnp.concatenate([skip_m, skip_o], 0)
    gain_m, gain_o = gain_m.astype(F32), gain_o.astype(F32)

    sources = (first, first_1, first_3, second, second_1, second_3, *first_2, *second_2)
    early, late, early_plan, late_plan = [], [], [], []
    for dz, dx in NEAR_SPOTS + FAR_SPOTS:
        spots = tuple(
            (base + {0: 0, 1: 1, 3: 2}[slow], fast) if slow != 2 else (base_far + fast // 2, fast % 2)
            for base, base_far, slow, fast in ((0, 6, dz, dx), (3, 8, dx, dz))
        )
        if len(early) < SLOTS:
            early.append((dz, dx))
            early_plan.append(spots)
        else:
            late.append((dz, dx))
            late_plan.append(spots)

    def chips_of(spots):
        back = jnp.array(spots, jnp.int32)
        return ((z - back[:, 0]) % RING) * RING + (x - back[:, 1]) % RING

    early_chip, late_chip = chips_of(early), chips_of(late)
    early_out, early_stat = far_first(
        early_plan, jnp.take(prefix_of, early_chip * 2 + core, axis=0), sources[:6], latents, latents_other
    )
    messages = far_second(
        late_plan,
        jnp.take(prefix_of, late_chip * 2 + core, axis=0),
        jnp.concatenate([early_chip, late_chip]),
        sources,
        latents,
        latents_other,
        w_uv,
        early_out,
        early_stat,
    )
    heads = combine(chip_exchange(messages), near_out, near_stat)
    head_out = chip_exchange(heads).reshape(CHIPS * DRAFT, HEADS * HD)
    hidden = skip.astype(F32) + exp_sum(project(head_out, w_out, w_out_o))
    hidden_rcv = swap_core(hidden)

    at = jnp.stack([core, z, x]).astype(jnp.int32)
    parts = gate_up(at, hidden, hidden_rcv, gain_m, gain_o, pick, pair_m, pair_o, shared_m, shared_o)
    gates, ups = parts[:RING], parts[RING:]
    gates_in = ring_send(gates[1:], X_BY)
    ups_in = ring_send(ups[1:], Z_BY)
    gates = fold([gates[0]] + gates_in)
    gates_in = ring_send(gates[1:], Z_BY)
    ups = fold([ups[0]] + ups_in)
    ups_in = ring_send(ups[1:], X_BY)
    acts = activate([gates[0]] + gates_in, [ups[0]] + ups_in, my_pick)
    mine, other = down(
        chip_exchange(acts), down_m, down_o, shared_down_m, shared_down_o, slot_weight, pick
    )
    mixed = exp_sum((mine + swap_core(other).astype(F32)).astype(BF))

    n = mine.shape[0]
    kept, other_half = hidden[:n], hidden_rcv[n:]
    hidden_m = jnp.where(
        core == 0, jnp.concatenate([kept, other_half], 1), jnp.concatenate([other_half, kept], 1)
    )
    return dot((hidden_m + mixed).astype(BF), to_order, NT).astype(BF).T


def solution(mesh):
    return jax.shard_map(
        per_device,
        mesh=mesh,
        in_specs=(
            P("pre", None, "exp", None),
            P("pre", None, None),
            P(None, "pre", None),
            P(),
            P(),
            P("exp", None, None),
            P("exp", "pre"),
            P(None, "pre"),
            P("pre"),
            P("exp", "pre", None, None),
            P("exp", None, "pre"),
            P("pre", None, "exp"),
            P("exp", "pre"),
            P(),
            P(),
        ),
        out_specs=P(None, "pre"),
        check_vma=False,
    )
```

time: 293 us -> 238 us (0.81)
  local copies, waits for them, and re-layouts: 76.2 us -> 27.8 us
  starting transfers between devices: 61.4 us -> 81.5 us
  waiting for transfers between devices: 90.5 us -> 73.6 us
  matrix products: 5.18 us -> 1.09 us
  other arithmetic: 8.27 us -> 4.43 us
    ppermute x8 -> x0, local copies, waits for them, and re-layouts: 22.9 us -> none  [the longest x6 12.3 us: ring_gather(): return [value] + [lax.ppermute(value, 'pre', pairs[d]) for d in (1, 2, 3)]]
    unnamed x75 -> x61, local copies, waits for them, and re-layouts: 29.8 us -> 7.09 us
    ppermute x12 -> x26, starting transfers between devices: 14.6 us -> 32 us  [the longest x18 20.7 us: ring_send(): lax.ppermute(value, 'pre', pairs[d])]
    all_to_all x4 -> x3, waiting for transfers between devices: 59.7 us -> 45.9 us  [chip_exchange(): return lax.all_to_all(value, 'pre', 0, 0, axis_index_groups=SAME_CORE)]
    another operation x9 -> x3, local copies, waits for them, and re-layouts: 10.1 us -> 0.12 us
    ppermute x10, starting transfers between devices: 18.3 us -> 25.6 us  [swap_core(): return lax.ppermute(value, 'pre', CORE)]
    optimization_barrier x0 -> x3, local copies, waits for them, and re-layouts: none -> 6.74 us  [the longest x2 5.31 us: per_device(): lax.optimization_barrier((first, w_out, residual, norm_gain, w_gate_up, w...]
    all_to_all x4 -> x3, starting transfers between devices: 19.1 us -> 14.3 us  [chip_exchange(): return lax.all_to_all(value, 'pre', 0, 0, axis_index_groups=SAME_CORE)]
  transfers between devices with their start and end apart: 32 -> 45, of which waited for: 10 -> 14; matrix products, arithmetic and copies ran while one was open for 26% -> 11% of each run, Pallas kernels for 4% -> 17%
where the time goes in v2:
time: 238 us; the launch traced here: 237 us
  starting transfers between devices  81.5 us (34%)
  waiting for transfers between devices  73.6 us (31%)
  Pallas kernels  48.1 us (20%)
  local copies, waits for them, and re-layouts  27.8 us (12%)
  other arithmetic  4.43 us (2%)
    all_to_all x3, waiting for transfers between devices, chip_exchange(): return lax.all_to_all(value, 'pre', 0, 0, axis_index_groups=SAME_CORE)  45.9 us
    ppermute x10, starting transfers between devices, swap_core(): return lax.ppermute(value, 'pre', CORE)  25.6 us
    ppermute x18, starting transfers between devices, ring_send(): lax.ppermute(value, 'pre', pairs[d])  20.7 us
    ppermute x18, waiting for transfers between devices, ring_send(): lax.ppermute(value, 'pre', pairs[d])  20.3 us
    pallas_call x1, Pallas kernels, far_second(): pl.pallas_call(functools.partial(far_second_kernel, plan), out_shape=shap...  17.2 us
    pallas_call x1, Pallas kernels, far_first(): pl.pallas_call(functools.partial(far_first_kernel, plan), out_shape=(shap...  14.5 us
    all_to_all x3, starting transfers between devices, chip_exchange(): return lax.all_to_all(value, 'pre', 0, 0, axis_index_groups=SAME_CORE)  14.3 us
    ppermute x6, starting transfers between devices, exp_sum(): lax.ppermute(value, 'exp', Y_BY[d]).astype(F32)  9.52 us
  transfers between devices with their start and end apart: 45, of which 14 were waited for; matrix products, arithmetic and copies ran while one was open for 11% of the time, Pallas kernels for 17%

profile of v2, /device:TPU:1, one launch (start us, length us, event | category | flops | bytes accessed | tf_op | source)
XLA Modules:
  0.0 237.3 jit_solution(10011224486453224239)
XLA Ops:
  4.9 3.3 %collective-permute-start.6 = (bf16[576,128]{1,0:T(8,128)(2,1)S(1)}, bf16[576,128]{1,0:T(8,128)(2,1)S(1)}, u32[]{:S(2)}, u32[]{:S(2)}) collective-permute-start(bf16[576,128]{1,0:T(8,128)(2,1)S(1)} %get-tuple-element.127), channel_id=1, source_target_pairs={{0,64},{4,68},{8,72},{12,76},{16,80},{20,84},{24,88},{28,92},{32,9... | collective-permute-start | bytes 442376 | tf_op jit(solution)/shard_map/ppermute | solution.py:61
  15.3 2.5 %collective-permute-start.1 = (bf16[576,128]{1,0:T(8,128)(2,1)S(1)}, bf16[576,128]{1,0:T(8,128)(2,1)S(1)}, u32[]{:S(2)}, u32[]{:S(2)}) collective-permute-start(bf16[576,128]{1,0:T(8,128)(2,1)S(1)} %get-tuple-element.129), channel_id=1, source_target_pairs={{0,16},{4,20},{8,24},{12,28},{16,0},{20,4},{24,8},{28,12},{32,48},... | collective-permute-start | bytes 442376 | tf_op jit(solution)/shard_map/ppermute | solution.py:61
  20.4 2.4 collective-permute-start.9
  28.1 5.3 %copy.82 = bf16[3,224,2,2048]{3,1,0,2:T(8,128)(2,1)S(1)} copy(bf16[3,224,2,2048]{3,2,1,0:T(2,128)(2,1)} %param.28) | data formatting | bytes 11010048 | tf_op jit(solution)/shard_map/optimization_barrier | solution.py:548
  37.9 2.2 dynamic-slice_bitcast_fusion
  40.3 2.9 %collective-permute-start.12 = (bf16[2,576,128]{2,1,0:T(8,128)(2,1)S(1)}, bf16[2,576,128]{2,1,0:T(8,128)(2,1)S(1)}, u32[]{:S(2)}, u32[]{:S(2)}) collective-permute-start(bf16[2,576,128]{2,1,0:T(8,128)(2,1)S(1)} %slice.75), channel_id=1, source_target_pairs={{0,96},{4,100},{8,104},{12,108},{16,112},{20,116},{24,120},{28,124... | collective-permute-start | bytes 884744 | tf_op jit(solution)/shard_map/ppermute | solution.py:586
  43.3 2.0 collective-permute-start.13
  46.2 4.7 %collective-permute-start.22 = (bf16[2,3,224,1024]{3,2,1,0:T(8,128)(2,1)}, bf16[2,3,224,1024]{3,2,1,0:T(8,128)(2,1)}, u32[]{:S(2)}, u32[]{:S(2)}) collective-permute-start(bf16[2,3,224,1024]{3,2,1,0:T(8,128)(2,1)} %get-tuple-element.85), channel_id=1, source_target_pairs={{0,4},{4,0},{8,12},{12,8},{16,20},{20,16},{24,28},{28,24},{32,36},... | collective-permute-start | bytes 8257544 | tf_op jit(solution)/shard_map/ppermute | solution.py:57
  50.8 14.5 %far_first.1 = (bf16[8,256,512]{2,1,0:T(8,128)(2,1)S(1)}, f32[8,8,128]{2,1,0:T(8,128)S(1)}) custom-call(s32[8]{0:T(128)S(1)} %and_select_fusion.prompt, bf16[4,576,128]{2,1,0:T(8,128)(2,1)S(1)} %pad_maximum_fusion.refs_0_, bf16[4,576,128]{2,1,0:T(8,128)(2,1)S(1)} %collective-permute-done.3.refs_1_, bf16[4,576,128]{2,1,0:T(8,128)(2,1)S(1)} %collective-permute-done.4.refs_2_, ...), custom_call_target="tpu_custom_call" | custom-call | flops 4563402752 | bytes 25165824 | tf_op jit(solution)/shard_map/far_first/pallas_call | solution.py:371
  65.4 17.2 %far_second.1 = bf16[16,272,128]{2,1,0:T(8,128)(2,1)S(1)} custom-call(s32[8]{0:T(128)S(1)} %and_select_fusion.1.prompt, s32[16]{0:T(128)S(1)} %pad_add_fusion.place, bf16[4,576,128]{2,1,0:T(8,128)(2,1)S(1)} %pad_maximum_fusion.refs_0_, bf16[4,576,128]{2,1,0:T(8,128)(2,1)S(1)} %collective-permute-done.3.refs_1_, ...), custom_call_target="tpu_custom_call" | custom-call | flops 4563402752 | bytes 25165824 | tf_op jit(solution)/shard_map/far_second/pallas_call | solution.py:389
  83.6 4.4 %all-to-all-start = ((bf16[16,272,128]{2,1,0:T(8,128)(2,1)}), bf16[16,272,128]{2,1,0:T(8,128)(2,1)}, u32[]{:S(2)}, u32[]{:S(2)}) async-start(bf16[16,272,128]{2,1,0:T(8,128)(2,1)} %copy-done.5), calls=%async_computation | async-start | bytes 2228224 | tf_op jit(solution)/shard_map/all_to_all | solution.py:70
  88.1 20.1 %all-to-all-done.rec_ref = bf16[16,272,128]{2,1,0:T(8,128)(2,1)} async-done(((bf16[16,272,128]{2,1,0:T(8,128)(2,1)}), bf16[16,272,128]{2,1,0:T(8,128)(2,1)}, u32[]{:S(2)}, u32[]{:S(2)}) %all-to-all-start) | async-done | bytes 1114144 | tf_op jit(solution)/shard_map/all_to_all | solution.py:70
  108.3 2.3 combine.1
  111.5 4.3 %all-to-all-start.1 = ((bf16[16,8,4096]{2,1,0:T(8,128)(2,1)}), bf16[16,8,4096]{2,1,0:T(8,128)(2,1)}, u32[]{:S(2)}, u32[]{:S(2)}) async-start(bf16[16,8,4096]{2,1,0:T(8,128)(2,1)} %copy-done.6), calls=%async_computation.1 | async-start | bytes 2097152 | tf_op jit(solution)/shard_map/all_to_all | solution.py:70
  115.8 16.2 %all-to-all-done.1 = bf16[16,8,4096]{2,1,0:T(8,128)(2,1)} async-done(((bf16[16,8,4096]{2,1,0:T(8,128)(2,1)}), bf16[16,8,4096]{2,1,0:T(8,128)(2,1)}, u32[]{:S(2)}, u32[]{:S(2)}) %all-to-all-start.1) | async-done | bytes 1048608 | tf_op jit(solution)/shard_map/all_to_all | solution.py:70
  133.5 3.6 %project.1 = bf16[448,128]{1,0:T(8,128)(2,1)S(1)} custom-call(bf16[128,4096]{1,0:T(8,128)(2,1)} %bitcast.48.head_ref, bf16[224,4096]{1,0:T(8,128)(2,1)S(1)} %bitcast.106, bf16[224,4096]{1,0:T(8,128)(2,1)} %collective-permute-done.16.wo_ref), custom_call_target="tpu_custom_call" | custom-call | tf_op jit(solution)/shard_map/project/pallas_call | solution.py:421
  137.1 2.9 %collective-permute-start.17 = (bf16[448,128]{1,0:T(8,128)(2,1)S(1)}, bf16[448,128]{1,0:T(8,128)(2,1)S(1)}, u32[]{:S(2)}, u32[]{:S(2)}) collective-permute-start(bf16[448,128]{1,0:T(8,128)(2,1)S(1)} %project.1), channel_id=1, source_target_pairs={{0,2},{1,3},{2,0},{3,1},{4,6},{5,7},{6,4},{7,5},{8,10},{9,11},{10,... | collective-permute-start | bytes 344072 | tf_op jit(solution)/shard_map/ppermute | solution.py:65
  140.5 2.3 collective-permute-start.19
  142.7 3.2 %collective-permute-start.10 = (bf16[224,128]{1,0:T(8,128)(2,1)S(1)}, bf16[224,128]{1,0:T(8,128)(2,1)S(1)}, u32[]{:S(2)}, u32[]{:S(2)}) collective-permute-start(bf16[224,128]{1,0:T(8,128)(2,1)S(1)} %get-tuple-element.70), channel_id=1, source_target_pairs={{0,4},{4,0},{8,12},{12,8},{16,20},{20,16},{24,28},{28,24},{32,36},... | collective-permute-start | bytes 172040 | tf_op jit(solution)/shard_map/ppermute | solution.py:57
  155.2 5.7 %gate_up.1 = (bf16[4,336,128]{2,1,0:T(8,128)(2,1)S(1)}, bf16[4,336,128]{2,1,0:T(8,128)(2,1)S(1)}, bf16[4,336,128]{2,1,0:T(8,128)(2,1)S(1)}, bf16[4,336,128]{2,1,...) custom-call(s32[3]{0:T(128)S(1)} %copy-done.11, ...), custom_call_target="tpu_custom_call" | custom-call | tf_op jit(solution)/shard_map/gate_up/pallas_call | solution.py:440
  165.4 12.7 %collective-permute-done.30.refs_1_ = bf16[4,320,128]{2,1,0:T(8,128)(2,1)S(1)} collective-permute-done((bf16[4,320,128]{2,1,0:T(8,128)(2,1)S(1)}, bf16[4,320,128]{2,1,0:T(8,128)(2,1)S(1)}, u32[]{:S(2)}, u32[]{:S(2)}) %collective-permute-start.30) | collective-permute-done | bytes 327712 | tf_op jit(solution)/shard_map/ppermute | solution.py:61
  179.8 2.9 %collective-permute-start.36 = (bf16[3,224,1024]{2,1,0:T(8,128)(2,1)}, bf16[3,224,1024]{2,1,0:T(8,128)(2,1)}, u32[]{:S(2)}, u32[]{:S(2)}) collective-permute-start(bf16[3,224,1024]{2,1,0:T(8,128)(2,1)} %get-tuple-element.106), channel_id=1, source_target_pairs={{0,4},{4,0},{8,12},{12,8},{16,20},{20,16},{24,28},{28,24},{32,36},... | collective-permute-start | bytes 4128776 | tf_op jit(solution)/shard_map/ppermute | solution.py:57
  182.7 3.7 %collective-permute-done.26.refs_3_ = bf16[4,336,128]{2,1,0:T(8,128)(2,1)S(1)} collective-permute-done((bf16[4,336,128]{2,1,0:T(8,128)(2,1)S(1)}, bf16[4,336,128]{2,1,0:T(8,128)(2,1)S(1)}, u32[]{:S(2)}, u32[]{:S(2)}) %collective-permute-start.26) | collective-permute-done | bytes 344096 | tf_op jit(solution)/shard_map/ppermute | solution.py:61
  188.1 2.0 collective-permute-start.29
  190.8 2.5 %collective-permute-done.35.refs_7_ = bf16[320,128]{1,0:T(8,128)(2,1)S(1)} collective-permute-done((bf16[320,128]{1,0:T(8,128)(2,1)S(1)}, bf16[320,128]{1,0:T(8,128)(2,1)S(1)}, u32[]{:S(2)}, u32[]{:S(2)}) %collective-permute-start.35) | collective-permute-done | bytes 81952 | tf_op jit(solution)/shard_map/ppermute | solution.py:61
  194.7 5.6 %all-to-all-start.2 = ((bf16[16,320,128]{2,1,0:T(8,128)(2,1)}), bf16[16,320,128]{2,1,0:T(8,128)(2,1)S(1)}, u32[]{:S(2)}, u32[]{:S(2)}) async-start(bf16[16,320,128]{2,1,0:T(8,128)(2,1)} %copy-done.4), calls=%async_computation.2 | async-start | bytes 2621440 | tf_op jit(solution)/shard_map/all_to_all | solution.py:70
  200.2 4.8 %collective-permute-start.37 = (bf16[224,256]{1,0:T(8,128)(2,1)}, bf16[224,256]{1,0:T(8,128)(2,1)S(1)}, u32[]{:S(2)}, u32[]{:S(2)}) collective-permute-start(bf16[224,256]{1,0:T(8,128)(2,1)} %get-tuple-element.108), channel_id=1, source_target_pairs={{0,4},{4,0},{8,12},{12,8},{16,20},{20,16},{24,28},{28,24},{32,36},... | collective-permute-start | bytes 344072 | tf_op jit(solution)/shard_map/ppermute | solution.py:57
  206.2 9.6 %all-to-all-done.2.act_ref = bf16[16,320,128]{2,1,0:T(8,128)(2,1)S(1)} async-done(((bf16[16,320,128]{2,1,0:T(8,128)(2,1)}), bf16[16,320,128]{2,1,0:T(8,128)(2,1)S(1)}, u32[]{:S(2)}, u32[]{:S(2)}) %all-to-all-start.2) | async-done | bytes 1310752 | tf_op jit(solution)/shard_map/all_to_all | solution.py:70
  216.7 3.2 %down.1 = (f32[224,256]{1,0:T(8,128)S(1)}, bf16[224,256]{1,0:T(8,128)(2,1)S(1)}) custom-call(bf16[16,320,128]{2,1,0:T(8,128)(2,1)S(1)} %all-to-all-done.2.act_ref, bf16[3,224,1024]{2,1,0:T(8,128)(2,1)S(1)} %copy-done.3, bf16[3,224,1024]{2,1,0:T(8,128)(2,1)} %collective-permute-done.36.wo_ref, bf16[224,256]{1,0:T(8,128)(2,1)S(1)} %copy-done.9, ...), custom_call_target="tpu_custom_call" | custom-call | tf_op jit(solution)/shard_map/down/pallas_call | solution.py:490
  219.9 6.4 %collective-permute-start.38 = (bf16[224,256]{1,0:T(8,128)(2,1)S(1)}, bf16[224,256]{1,0:T(8,128)(2,1)S(1)}, u32[]{:S(2)}, u32[]{:S(2)}) collective-permute-start(bf16[224,256]{1,0:T(8,128)(2,1)S(1)} %get-tuple-element.111), channel_id=1, source_target_pairs={{0,4},{4,0},{8,12},{12,8},{16,20},{20,16},{24,28},{28,24},{32,36},... | collective-permute-start | bytes 344072 | tf_op jit(solution)/shard_map/ppermute | solution.py:57
  228.5 2.4 %collective-permute-start.40 = (bf16[224,256]{1,0:T(8,128)(2,1)S(1)}, bf16[224,256]{1,0:T(8,128)(2,1)S(1)}, u32[]{:S(2)}, u32[]{:S(2)}) collective-permute-start(bf16[224,256]{1,0:T(8,128)(2,1)S(1)} %add_convert_fusion), channel_id=1, source_target_pairs={{0,1},{1,2},{2,3},{3,0},{4,5},{5,6},{6,7},{7,4},{8,9},{9,10},{10,1... | collective-permute-start | bytes 344072 | tf_op jit(solution)/shard_map/ppermute | solution.py:65
  233.3 3.1 %collective-permute-done.40 = bf16[224,256]{1,0:T(8,128)(2,1)S(1)} collective-permute-done((bf16[224,256]{1,0:T(8,128)(2,1)S(1)}, bf16[224,256]{1,0:T(8,128)(2,1)S(1)}, u32[]{:S(2)}, u32[]{:S(2)}) %collective-permute-start.40) | collective-permute-done | bytes 114720 | tf_op jit(solution)/shard_map/ppermute | solution.py:65
  (212 shorter events, 55.6 us)
Async XLA Ops:
  0.1 46.1 %collective-permute-start.15 = (bf16[8,576,512]{2,1,0:T(8,128)(2,1)}, bf16[8,576,512]{2,1,0:T(8,128)(2,1)}, u32[]{:S(2)}, u32[]{:S(2)}) collective-permute-start(bf16[8,576,512]{2,1,0:T(8,128)(2,1)} %bitcast.100), channel_id=1, source_target_pairs={{0,4},{4,0},{8,12},{12,8},{16,20},{20,16},{24,28},{28,24},{32,36},... | collective-permute-start | bytes 14155784 | tf_op jit(solution)/shard_map/ppermute | solution.py:57
  3.1 12.2 %collective-permute-start.5 = (bf16[576,128]{1,0:T(8,128)(2,1)S(1)}, bf16[576,128]{1,0:T(8,128)(2,1)S(1)}, u32[]{:S(2)}, u32[]{:S(2)}) collective-permute-start(bf16[576,128]{1,0:T(8,128)(2,1)S(1)} %get-tuple-element.127), channel_id=1, source_target_pairs={{0,32},{4,36},{8,40},{12,44},{16,48},{20,52},{24,56},{28,60},{32,6... | collective-permute-start | bytes 442376 | tf_op jit(solution)/shard_map/ppermute | solution.py:61
  4.9 12.9 %collective-permute-start.6 = (bf16[576,128]{1,0:T(8,128)(2,1)S(1)}, bf16[576,128]{1,0:T(8,128)(2,1)S(1)}, u32[]{:S(2)}, u32[]{:S(2)}) collective-permute-start(bf16[576,128]{1,0:T(8,128)(2,1)S(1)} %get-tuple-element.127), channel_id=1, source_target_pairs={{0,64},{4,68},{8,72},{12,76},{16,80},{20,84},{24,88},{28,92},{32,9... | collective-permute-start | bytes 442376 | tf_op jit(solution)/shard_map/ppermute | solution.py:61
  8.3 11.6 %collective-permute-start.7 = (bf16[576,128]{1,0:T(8,128)(2,1)S(1)}, bf16[576,128]{1,0:T(8,128)(2,1)S(1)}, u32[]{:S(2)}, u32[]{:S(2)}) collective-permute-start(bf16[576,128]{1,0:T(8,128)(2,1)S(1)} %get-tuple-element.127), channel_id=1, source_target_pairs={{0,96},{4,100},{8,104},{12,108},{16,112},{20,116},{24,120},{28,124... | collective-permute-start | bytes 442376 | tf_op jit(solution)/shard_map/ppermute | solution.py:61
  9.5 10.9 %collective-permute-start = (bf16[576,128]{1,0:T(8,128)(2,1)S(1)}, bf16[576,128]{1,0:T(8,128)(2,1)S(1)}, u32[]{:S(2)}, u32[]{:S(2)}) collective-permute-start(bf16[576,128]{1,0:T(8,128)(2,1)S(1)} %get-tuple-element.129), channel_id=1, source_target_pairs={{0,8},{4,12},{8,16},{12,20},{16,24},{20,28},{24,0},{28,4},{32,40},... | collective-permute-start | bytes 442376 | tf_op jit(solution)/shard_map/ppermute | solution.py:61
  15.3 7.4 %collective-permute-start.1 = (bf16[576,128]{1,0:T(8,128)(2,1)S(1)}, bf16[576,128]{1,0:T(8,128)(2,1)S(1)}, u32[]{:S(2)}, u32[]{:S(2)}) collective-permute-start(bf16[576,128]{1,0:T(8,128)(2,1)S(1)} %get-tuple-element.129), channel_id=1, source_target_pairs={{0,16},{4,20},{8,24},{12,28},{16,0},{20,4},{24,8},{28,12},{32,48},... | collective-permute-start | bytes 442376 | tf_op jit(solution)/shard_map/ppermute | solution.py:61
  20.0 20.2 %collective-permute-start.8 = (bf16[4,576,128]{2,1,0:T(8,128)(2,1)S(1)}, bf16[4,576,128]{2,1,0:T(8,128)(2,1)S(1)}, u32[]{:S(2)}, u32[]{:S(2)}) collective-permute-start(bf16[4,576,128]{2,1,0:T(8,128)(2,1)S(1)} %pad_maximum_fusion.1.refs_3_), channel_id=1, source_target_pairs={{0,8},{4,12},{8,16},{12,20},{16,24},{20,28},{24,0},{28,4},{32,40},... | collective-permute-start | bytes 1769480 | tf_op jit(solution)/shard_map/ppermute | solution.py:546
  20.4 19.8 %collective-permute-start.9 = (bf16[4,576,128]{2,1,0:T(8,128)(2,1)S(1)}, bf16[4,576,128]{2,1,0:T(8,128)(2,1)S(1)}, u32[]{:S(2)}, u32[]{:S(2)}) collective-permute-start(bf16[4,576,128]{2,1,0:T(8,128)(2,1)S(1)} %pad_maximum_fusion.1.refs_3_), channel_id=1, source_target_pairs={{0,24},{4,28},{8,0},{12,4},{16,8},{20,12},{24,16},{28,20},{32,56},... | collective-permute-start | bytes 1769480 | tf_op jit(solution)/shard_map/ppermute | solution.py:546
  23.8 16.4 %collective-permute-start.3 = (bf16[4,576,128]{2,1,0:T(8,128)(2,1)S(1)}, bf16[4,576,128]{2,1,0:T(8,128)(2,1)S(1)}, u32[]{:S(2)}, u32[]{:S(2)}) collective-permute-start(bf16[4,576,128]{2,1,0:T(8,128)(2,1)S(1)} %pad_maximum_fusion.refs_0_), channel_id=1, source_target_pairs={{0,32},{4,36},{8,40},{12,44},{16,48},{20,52},{24,56},{28,60},{32,6... | collective-permute-start | bytes 1769480 | tf_op jit(solution)/shard_map/ppermute | solution.py:545
  24.6 15.6 %collective-permute-start.4 = (bf16[4,576,128]{2,1,0:T(8,128)(2,1)S(1)}, bf16[4,576,128]{2,1,0:T(8,128)(2,1)S(1)}, u32[]{:S(2)}, u32[]{:S(2)}) collective-permute-start(bf16[4,576,128]{2,1,0:T(8,128)(2,1)S(1)} %pad_maximum_fusion.refs_0_), channel_id=1, source_target_pairs={{0,96},{4,100},{8,104},{12,108},{16,112},{20,116},{24,120},{28,124... | collective-permute-start | bytes 1769480 | tf_op jit(solution)/shard_map/ppermute | solution.py:545
  40.2 25.1 %collective-permute-start.11 = (bf16[2,576,128]{2,1,0:T(8,128)(2,1)S(1)}, bf16[2,576,128]{2,1,0:T(8,128)(2,1)S(1)}, u32[]{:S(2)}, u32[]{:S(2)}) collective-permute-start(bf16[2,576,128]{2,1,0:T(8,128)(2,1)S(1)} %slice.74), channel_id=1, source_target_pairs={{0,32},{4,36},{8,40},{12,44},{16,48},{20,52},{24,56},{28,60},{32,6... | collective-permute-start | bytes 884744 | tf_op jit(solution)/shard_map/ppermute | solution.py:586
  40.3 25.0 %collective-permute-start.12 = (bf16[2,576,128]{2,1,0:T(8,128)(2,1)S(1)}, bf16[2,576,128]{2,1,0:T(8,128)(2,1)S(1)}, u32[]{:S(2)}, u32[]{:S(2)}) collective-permute-start(bf16[2,576,128]{2,1,0:T(8,128)(2,1)S(1)} %slice.75), channel_id=1, source_target_pairs={{0,96},{4,100},{8,104},{12,108},{16,112},{20,116},{24,120},{28,124... | collective-permute-start | bytes 884744 | tf_op jit(solution)/shard_map/ppermute | solution.py:586
  43.3 22.1 %collective-permute-start.13 = (bf16[2,576,128]{2,1,0:T(8,128)(2,1)S(1)}, bf16[2,576,128]{2,1,0:T(8,128)(2,1)S(1)}, u32[]{:S(2)}, u32[]{:S(2)}) collective-permute-start(bf16[2,576,128]{2,1,0:T(8,128)(2,1)S(1)} %slice.76), channel_id=1, source_target_pairs={{0,8},{4,12},{8,16},{12,20},{16,24},{20,28},{24,0},{28,4},{32,40},... | collective-permute-start | bytes 884744 | tf_op jit(solution)/shard_map/ppermute | solution.py:587
  45.3 20.1 %collective-permute-start.14 = (bf16[2,576,128]{2,1,0:T(8,128)(2,1)S(1)}, bf16[2,576,128]{2,1,0:T(8,128)(2,1)S(1)}, u32[]{:S(2)}, u32[]{:S(2)}) collective-permute-start(bf16[2,576,128]{2,1,0:T(8,128)(2,1)S(1)} %slice.77), channel_id=1, source_target_pairs={{0,24},{4,28},{8,0},{12,4},{16,8},{20,12},{24,16},{28,20},{32,56},... | collective-permute-start | bytes 884744 | tf_op jit(solution)/shard_map/ppermute | solution.py:587
  46.2 107.4 %collective-permute-start.22 = (bf16[2,3,224,1024]{3,2,1,0:T(8,128)(2,1)}, bf16[2,3,224,1024]{3,2,1,0:T(8,128)(2,1)}, u32[]{:S(2)}, u32[]{:S(2)}) collective-permute-start(bf16[2,3,224,1024]{3,2,1,0:T(8,128)(2,1)} %get-tuple-element.85), channel_id=1, source_target_pairs={{0,4},{4,0},{8,12},{12,8},{16,20},{20,16},{24,28},{28,24},{32,36},... | collective-permute-start | bytes 8257544 | tf_op jit(solution)/shard_map/ppermute | solution.py:57
  83.6 24.6 %all-to-all-start = ((bf16[16,272,128]{2,1,0:T(8,128)(2,1)}), bf16[16,272,128]{2,1,0:T(8,128)(2,1)}, u32[]{:S(2)}, u32[]{:S(2)}) async-start(bf16[16,272,128]{2,1,0:T(8,128)(2,1)} %copy-done.5), calls=%async_computation | async-start | bytes 2228224 | tf_op jit(solution)/shard_map/all_to_all | solution.py:70
  88.0 27.8 %collective-permute-start.16 = (bf16[224,4096]{1,0:T(8,128)(2,1)}, bf16[224,4096]{1,0:T(8,128)(2,1)}, u32[]{:S(2)}, u32[]{:S(2)}) collective-permute-start(bf16[224,4096]{1,0:T(8,128)(2,1)} %bitcast.105), channel_id=1, source_target_pairs={{0,4},{4,0},{8,12},{12,8},{16,20},{20,16},{24,28},{28,24},{32,36},... | collective-permute-start | bytes 5505032 | tf_op jit(solution)/shard_map/ppermute | solution.py:57
  111.5 20.5 %all-to-all-start.1 = ((bf16[16,8,4096]{2,1,0:T(8,128)(2,1)}), bf16[16,8,4096]{2,1,0:T(8,128)(2,1)}, u32[]{:S(2)}, u32[]{:S(2)}) async-start(bf16[16,8,4096]{2,1,0:T(8,128)(2,1)} %copy-done.6), calls=%async_computation.1 | async-start | bytes 2097152 | tf_op jit(solution)/shard_map/all_to_all | solution.py:70
  137.1 10.1 %collective-permute-start.17 = (bf16[448,128]{1,0:T(8,128)(2,1)S(1)}, bf16[448,128]{1,0:T(8,128)(2,1)S(1)}, u32[]{:S(2)}, u32[]{:S(2)}) collective-permute-start(bf16[448,128]{1,0:T(8,128)(2,1)S(1)} %project.1), channel_id=1, source_target_pairs={{0,2},{1,3},{2,0},{3,1},{4,6},{5,7},{6,4},{7,5},{8,10},{9,11},{10,... | collective-permute-start | bytes 344072 | tf_op jit(solution)/shard_map/ppermute | solution.py:65
  140.1 7.2 %collective-permute-start.18 = (bf16[448,128]{1,0:T(8,128)(2,1)S(1)}, bf16[448,128]{1,0:T(8,128)(2,1)S(1)}, u32[]{:S(2)}, u32[]{:S(2)}) collective-permute-start(bf16[448,128]{1,0:T(8,128)(2,1)S(1)} %project.1), channel_id=1, source_target_pairs={{0,1},{1,2},{2,3},{3,0},{4,5},{5,6},{6,7},{7,4},{8,9},{9,10},{10,1... | collective-permute-start | bytes 344072 | tf_op jit(solution)/shard_map/ppermute | solution.py:65
  160.9 17.2 %collective-permute-start.30 = (bf16[4,320,128]{2,1,0:T(8,128)(2,1)S(1)}, bf16[4,320,128]{2,1,0:T(8,128)(2,1)S(1)}, u32[]{:S(2)}, u32[]{:S(2)}) collective-permute-start(bf16[4,320,128]{2,1,0:T(8,128)(2,1)S(1)} %get-tuple-element.97), channel_id=1, source_target_pairs={{0,32},{4,36},{8,40},{12,44},{16,48},{20,52},{24,56},{28,60},{32,6... | collective-permute-start | bytes 983048 | tf_op jit(solution)/shard_map/ppermute | solution.py:61
  161.0 17.1 %collective-permute-start.31 = (bf16[4,320,128]{2,1,0:T(8,128)(2,1)S(1)}, bf16[4,320,128]{2,1,0:T(8,128)(2,1)S(1)}, u32[]{:S(2)}, u32[]{:S(2)}) collective-permute-start(bf16[4,320,128]{2,1,0:T(8,128)(2,1)S(1)} %get-tuple-element.98), channel_id=1, source_target_pairs={{0,64},{4,68},{8,72},{12,76},{16,80},{20,84},{24,88},{28,92},{32,9... | collective-permute-start | bytes 983048 | tf_op jit(solution)/shard_map/ppermute | solution.py:61
  162.2 16.2 %collective-permute-start.32 = (bf16[4,320,128]{2,1,0:T(8,128)(2,1)S(1)}, bf16[4,320,128]{2,1,0:T(8,128)(2,1)S(1)}, u32[]{:S(2)}, u32[]{:S(2)}) collective-permute-start(bf16[4,320,128]{2,1,0:T(8,128)(2,1)S(1)} %get-tuple-element.99), channel_id=1, source_target_pairs={{0,96},{4,100},{8,104},{12,108},{16,112},{20,116},{24,120},{28,124... | collective-permute-start | bytes 983048 | tf_op jit(solution)/shard_map/ppermute | solution.py:61
  163.6 16.1 %collective-permute-start.24 = (bf16[4,336,128]{2,1,0:T(8,128)(2,1)S(1)}, bf16[4,336,128]{2,1,0:T(8,128)(2,1)S(1)}, u32[]{:S(2)}, u32[]{:S(2)}) collective-permute-start(bf16[4,336,128]{2,1,0:T(8,128)(2,1)S(1)} %get-tuple-element.89), channel_id=1, source_target_pairs={{0,8},{4,12},{8,16},{12,20},{16,24},{20,28},{24,0},{28,4},{32,40},... | collective-permute-start | bytes 1032200 | tf_op jit(solution)/shard_map/ppermute | solution.py:61
  163.6 19.1 %collective-permute-start.25 = (bf16[4,336,128]{2,1,0:T(8,128)(2,1)S(1)}, bf16[4,336,128]{2,1,0:T(8,128)(2,1)S(1)}, u32[]{:S(2)}, u32[]{:S(2)}) collective-permute-start(bf16[4,336,128]{2,1,0:T(8,128)(2,1)S(1)} %get-tuple-element.90), channel_id=1, source_target_pairs={{0,16},{4,20},{8,24},{12,28},{16,0},{20,4},{24,8},{28,12},{32,48},... | collective-permute-start | bytes 1032200 | tf_op jit(solution)/shard_map/ppermute | solution.py:61
  178.1 8.3 %collective-permute-start.26 = (bf16[4,336,128]{2,1,0:T(8,128)(2,1)S(1)}, bf16[4,336,128]{2,1,0:T(8,128)(2,1)S(1)}, u32[]{:S(2)}, u32[]{:S(2)}) collective-permute-start(bf16[4,336,128]{2,1,0:T(8,128)(2,1)S(1)} %get-tuple-element.91), channel_id=1, source_target_pairs={{0,24},{4,28},{8,0},{12,4},{16,8},{20,12},{24,16},{28,20},{32,56},... | collective-permute-start | bytes 1032200 | tf_op jit(solution)/shard_map/ppermute | solution.py:61
  178.6 9.5 %collective-permute-start.33 = (bf16[320,128]{1,0:T(8,128)(2,1)S(1)}, bf16[320,128]{1,0:T(8,128)(2,1)S(1)}, u32[]{:S(2)}, u32[]{:S(2)}) collective-permute-start(bf16[320,128]{1,0:T(8,128)(2,1)S(1)} %get-tuple-element.101), channel_id=1, source_target_pairs={{0,8},{4,12},{8,16},{12,20},{16,24},{20,28},{24,0},{28,4},{32,40},... | collective-permute-start | bytes 245768 | tf_op jit(solution)/shard_map/ppermute | solution.py:61
  179.8 10.3 %collective-permute-start.34 = (bf16[320,128]{1,0:T(8,128)(2,1)S(1)}, bf16[320,128]{1,0:T(8,128)(2,1)S(1)}, u32[]{:S(2)}, u32[]{:S(2)}) collective-permute-start(bf16[320,128]{1,0:T(8,128)(2,1)S(1)} %get-tuple-element.102), channel_id=1, source_target_pairs={{0,16},{4,20},{8,24},{12,28},{16,0},{20,4},{24,8},{28,12},{32,48},... | collective-permute-start | bytes 245768 | tf_op jit(solution)/shard_map/ppermute | solution.py:61
  179.8 26.5 %collective-permute-start.36 = (bf16[3,224,1024]{2,1,0:T(8,128)(2,1)}, bf16[3,224,1024]{2,1,0:T(8,128)(2,1)}, u32[]{:S(2)}, u32[]{:S(2)}) collective-permute-start(bf16[3,224,1024]{2,1,0:T(8,128)(2,1)} %get-tuple-element.106), channel_id=1, source_target_pairs={{0,4},{4,0},{8,12},{12,8},{16,20},{20,16},{24,28},{28,24},{32,36},... | collective-permute-start | bytes 4128776 | tf_op jit(solution)/shard_map/ppermute | solution.py:57
  194.7 21.1 %all-to-all-start.2 = ((bf16[16,320,128]{2,1,0:T(8,128)(2,1)}), bf16[16,320,128]{2,1,0:T(8,128)(2,1)S(1)}, u32[]{:S(2)}, u32[]{:S(2)}) async-start(bf16[16,320,128]{2,1,0:T(8,128)(2,1)} %copy-done.4), calls=%async_computation.2 | async-start | bytes 2621440 | tf_op jit(solution)/shard_map/all_to_all | solution.py:70
  219.9 7.4 %collective-permute-start.38 = (bf16[224,256]{1,0:T(8,128)(2,1)S(1)}, bf16[224,256]{1,0:T(8,128)(2,1)S(1)}, u32[]{:S(2)}, u32[]{:S(2)}) collective-permute-start(bf16[224,256]{1,0:T(8,128)(2,1)S(1)} %get-tuple-element.111), channel_id=1, source_target_pairs={{0,4},{4,0},{8,12},{12,8},{16,20},{20,16},{24,28},{28,24},{32,36},... | collective-permute-start | bytes 344072 | tf_op jit(solution)/shard_map/ppermute | solution.py:57
  228.5 7.8 %collective-permute-start.40 = (bf16[224,256]{1,0:T(8,128)(2,1)S(1)}, bf16[224,256]{1,0:T(8,128)(2,1)S(1)}, u32[]{:S(2)}, u32[]{:S(2)}) collective-permute-start(bf16[224,256]{1,0:T(8,128)(2,1)S(1)} %add_convert_fusion), channel_id=1, source_target_pairs={{0,1},{1,2},{2,3},{3,0},{4,5},{5,6},{6,7},{7,4},{8,9},{9,10},{10,1... | collective-permute-start | bytes 344072 | tf_op jit(solution)/shard_map/ppermute | solution.py:65
  (43 other events, 434.7 us)
